TPU v7x, 32 devices: a whole 2x2x4 slice. The times are simulated.
32 devices in a mesh: wide: 8 (over z, core), narrow: 4 (over y, x).
Axes of the slice: x: 2, y: 2, z: 4, core: 2. Of those that a mesh axis runs over, the one named last changes fastest.
Arguments:
- fields: float32 [5, 8, 32, 256], P(None, 'wide', 'narrow'), may hold values from -2.1 to 6.1, as said below
- prior_modes: bfloat16 [124, 5, 8, 8192], P(None, None, 'wide', 'narrow'), may hold values from -360 to 360, as said below
Outputs:
- flow_state: float32 [5, 8, 32, 256], P(None, 'wide', 'narrow')
- factor: float32 [128, 128], replicated
Inputs may be any that keep to these rules, and one draw needn't show every extreme that they name: `fields`: density and pressure lie in 0.6 to 1.4, each velocity component below 1.5 in magnitude. `prior_modes`: the columns are linearly independent.
All inputs are finite; a program needn't handle non-finite values.
Results may differ from a plain program's by a relative error of at most 0.0014.
Values may be sent and summed in bfloat16 or wider, within the bound.
A program may use at most 64 MiB of HBM per device.

v0:
```python
import jax
import jax.numpy as jnp
from jax import lax
from jax.sharding import PartitionSpec as P

STEPS = 2


GAMMA = 1.4
TIME_STEP = 0.25
VISCOSITY = 0.15


def extended(block, sides, width):
    for axis, dim in sides:
        count = lax.axis_size(axis)
        forward = [(i, i + 1) for i in range(count - 1)]
        forward.append((count - 1, 0))
        backward = [(target, source) for source, target in forward]
        low = lax.ppermute(
            lax.slice_in_dim(block, block.shape[dim] - width, None, axis=dim), axis, forward
        )
        high = lax.ppermute(lax.slice_in_dim(block, 0, width, axis=dim), axis, backward)
        block = jnp.concatenate([low, block, high], axis=dim)
    return block


def flux_of(current, dim_index):
    density = current[0]
    momentum = current[1:4]
    energy = current[4]
    vel_d = momentum[dim_index] / density
    pressure = (GAMMA - 1.0) * (
        energy
        - 0.5
        * (momentum[0] * momentum[0] + momentum[1] * momentum[1] + momentum[2] * momentum[2])
        / density
    )
    components = [
        momentum[dim_index],
        momentum[0] * vel_d,
        momentum[1] * vel_d,
        momentum[2] * vel_d,
        (energy + pressure) * vel_d,
    ]
    components[1 + dim_index] = components[1 + dim_index] + pressure
    return jnp.stack(components)


def tendency(current):
    padded = extended(current.astype(jnp.bfloat16), (("wide", 1), ("narrow", 2)), 1).astype(
        current.dtype
    )
    flux_x = flux_of(padded[:, :, 1:-1], 0)
    flux_y = flux_of(padded[:, 1:-1, :], 1)
    flux_z = flux_of(current, 2)
    divergence = (
        flux_x[:, 2:]
        - flux_x[:, :-2]
        + (flux_y[:, :, 2:] - flux_y[:, :, :-2])
        + (jnp.roll(flux_z, -1, 3) - jnp.roll(flux_z, 1, 3))
    )
    laplace = (
        padded[:, 2:, 1:-1]
        + padded[:, :-2, 1:-1]
        + padded[:, 1:-1, 2:]
        + padded[:, 1:-1, :-2]
        + jnp.roll(current, -1, 3)
        + jnp.roll(current, 1, 3)
        - 6.0 * current
    )
    return -0.5 * divergence + VISCOSITY * laplace


def local(fields, prior_modes):
    wide_count = lax.axis_size("wide")
    narrow_count = lax.axis_size("narrow")
    cells_x, cells_y, cells_z = (fields.shape[1], fields.shape[2], fields.shape[3])
    inverse_cells = 1.0 / (cells_x * wide_count * cells_y * narrow_count * cells_z)
    flat_modes = prior_modes.reshape(prior_modes.shape[0], -1)
    contract = (((1,), (1,)), ((), ()))
    gram_modes = lax.dot_general(
        flat_modes, flat_modes, contract, preferred_element_type=jnp.float32
    )
    current = fields
    snapshots = []
    for step_index in range(STEPS):
        section_one = current + TIME_STEP * tendency(current)
        snapshots.append(section_one.astype(jnp.bfloat16))
        current = 0.5 * current + 0.5 * (section_one + TIME_STEP * tendency(section_one))
        snapshots.append(current.astype(jnp.bfloat16))
    arrived = lax.all_to_all(
        jnp.stack(snapshots), "narrow", split_axis=4, concat_axis=3, tiled=True
    )
    snap_rows = jnp.swapaxes(arrived, 3, 4).reshape(arrived.shape[0], -1)
    cross_gram = lax.dot_general(
        flat_modes, snap_rows, contract, preferred_element_type=jnp.float32
    )
    snap_gram = lax.dot_general(snap_rows, snap_rows, contract, preferred_element_type=jnp.float32)
    gram_local = jnp.concatenate(
        [
            jnp.concatenate([gram_modes, cross_gram], 1),
            jnp.concatenate([cross_gram.T, snap_gram], 1),
        ],
        0,
    )
    gram_local = gram_local * inverse_cells
    gram_whole = lax.psum(gram_local, ("wide", "narrow"))
    factor = jnp.linalg.cholesky(gram_whole).T
    return (current, factor)


def solution(mesh):
    placed = (P(None, "wide", "narrow", None), P(None, None, "wide", "narrow"))
    return jax.shard_map(
        local,
        mesh=mesh,
        in_specs=placed,
        out_specs=(P(None, "wide", "narrow", None), P()),
        check_vma=False,
    )
```

profile of v0, /device:TPU:0, one launch (start us, length us, event | category | flops | bytes accessed | tf_op | source)
XLA Modules:
  0.0 218.9 jit_solution(10994028326909656914)
XLA Ops:
  7.2 0.8 convert_element_type.30
  7.9 4.5 %collective-permute-start.1 = (bf16[5,1,8,256]{3,2,1,0:T(8,128)(2,1)S(1)}, bf16[5,1,8,256]{3,2,1,0:T(8,128)(2,1)S(1)}, u32[]{:S(2)}, u32[]{:S(2)}) collective-permute-start(bf16[5,1,8,256]{3,2,1,0:T(8,128)(2,1)S(1)} %convert_element_type.30), channel_id=1, source_target_pairs={{4,0},{8,4},{12,8},{16,12},{20,16},{24,20},{28,24},{0,28},{5,1},{9... | collective-permute-start | bytes 61448 | tf_op jit(solution)/shard_map/ppermute | solution.py:23
  12.4 0.7 constant_dynamic-update-slice_fusion.14
  13.1 0.8 constant_dynamic-update-slice_fusion.13
  13.9 0.7 constant_dynamic-update-slice_fusion.12
  14.6 0.8 constant_dynamic-update-slice_fusion.11
  15.4 0.7 constant_dynamic-update-slice_fusion.10
  16.1 0.9 fusion.97
  17.1 0.4 collective-permute-done
  17.5 2.5 %collective-permute-start.3 = (bf16[5,3,1,256]{3,1,2,0:T(4,128)(2,1)S(1)}, bf16[5,3,1,256]{3,1,2,0:T(4,128)(2,1)S(1)}, u32[]{:S(2)}, u32[]{:S(2)}) collective-permute-start(bf16[5,3,1,256]{3,1,2,0:T(4,128)(2,1)S(1)} %copy.422), channel_id=1, source_target_pairs={{1,0},{2,1},{3,2},{0,3},{5,4},{6,5},{7,6},{4,7},{9,8},{10,9},{11,1... | collective-permute-start | bytes 23048 | tf_op jit(solution)/shard_map/ppermute | solution.py:23
  20.0 0.8 fusion.98
  20.8 0.5 collective-permute-done.3
  21.4 3.2 %collective-permute-done.2 = bf16[5,3,1,256]{3,1,2,0:T(4,128)(2,1)S(1)} collective-permute-done((bf16[5,3,1,256]{3,1,2,0:T(4,128)(2,1)S(1)}, bf16[5,3,1,256]{3,1,2,0:T(4,128)(2,1)S(1)}, u32[]{:S(2)}, u32[]{:S(2)}) %collective-permute-start.2) | collective-permute-done | bytes 7712 | tf_op jit(solution)/shard_map/ppermute | solution.py:20
  24.9 0.9 fusion.82
  25.8 1.8 collective-permute-start.5
  27.7 0.1 fusion.93
  27.9 1.2 collective-permute-done.5
  29.1 3.5 %collective-permute-done.4 = bf16[5,1,8,256]{3,2,0,1:T(8,128)(2,1)S(1)} collective-permute-done((bf16[5,1,8,256]{3,2,0,1:T(8,128)(2,1)S(1)}, bf16[5,1,8,256]{3,2,0,1:T(8,128)(2,1)S(1)}, u32[]{:S(2)}, u32[]{:S(2)}) %collective-permute-start.4) | collective-permute-done | bytes 20512 | tf_op jit(solution)/shard_map/ppermute | solution.py:20
  32.6 0.4 collective-permute-start.7
  33.0 1.7 collective-permute-start.6
  34.8 1.6 collective-permute-done.7
  36.4 1.2 collective-permute-done.6
  37.9 0.1 broadcast_multiply_fusion
  38.0 0.1 fusion.91
  38.2 0.5 collective-permute-start.8
  38.8 0.1 fusion.89
  38.9 0.8 collective-permute-done.9
  39.7 3.6 %collective-permute-done.8 = bf16[5,1,8,256]{3,2,0,1:T(8,128)(2,1)S(1)} collective-permute-done((bf16[5,1,8,256]{3,2,0,1:T(8,128)(2,1)S(1)}, bf16[5,1,8,256]{3,2,0,1:T(8,128)(2,1)S(1)}, u32[]{:S(2)}, u32[]{:S(2)}) %collective-permute-start.8) | collective-permute-done | bytes 20512 | tf_op jit(solution)/shard_map/ppermute | solution.py:20
  43.3 0.8 collective-permute-start.11
  44.1 1.3 collective-permute-start.10
  45.4 1.6 collective-permute-done.11
  47.1 1.7 collective-permute-done.10
  49.0 0.1 fusion.79
  49.2 0.5 collective-permute-start.12
  49.8 0.1 fusion.85
  50.0 0.7 collective-permute-done.13
  50.7 3.6 %collective-permute-done.12 = bf16[5,1,8,256]{3,2,0,1:T(8,128)(2,1)S(1)} collective-permute-done((bf16[5,1,8,256]{3,2,0,1:T(8,128)(2,1)S(1)}, bf16[5,1,8,256]{3,2,0,1:T(8,128)(2,1)S(1)}, u32[]{:S(2)}, u32[]{:S(2)}) %collective-permute-start.12) | collective-permute-done | bytes 20512 | tf_op jit(solution)/shard_map/ppermute | solution.py:20
  54.3 0.5 collective-permute-start.15
  54.8 1.6 collective-permute-start.14
  56.5 1.6 collective-permute-done.15
  58.1 1.3 collective-permute-done.14
  59.7 0.7 convert_bitcast_fusion
  60.4 0.7 copy.412
  61.2 2.1 reshape.630
  63.2 3.3 %all-to-all-start = ((bf16[4,2,5120]{2,1,0:T(2,128)(2,1)}), bf16[4,2,5120]{2,1,0:T(2,128)(2,1)S(1)}, u32[]{:S(2)}, u32[]{:S(2)}) async-start(bf16[4,2,5120]{2,1,0:T(2,128)(2,1)} %reshape.630), calls=%async_computation | async-start | bytes 163840 | tf_op jit(solution)/shard_map/all_to_all | solution.py:92
  66.5 0.2 all-reduce.2.cloned.1.call-start
  66.8 3.4 %fusion.2 = f32[124,124]{0,1:T(8,128)S(1)} fusion(bf16[124,5,1,2048]{3,0,2,1:T(8,128)(2,1)} %param.3), kind=kOutput, calls=%fused_computation.2 | convolution fusion | flops 314900480 | bytes 2601024 | tf_op jit(solution)/shard_map/dot_general | solution.py:82
  70.1 3.3 %copy.415 = bf16[124,5,1,2048]{0,3,1,2:T(8,128)(2,1)S(1)} copy(bf16[124,5,1,2048]{3,0,2,1:T(8,128)(2,1)} %param.3) | data formatting | bytes 5079040 | tf_op args[1]
  73.5 2.6 %reshape.631 = bf16[256,5,1,4,8]{4,3,2,1,0:T(4,128)(2,1)} reshape(bf16[4,2,5120]{2,1,0:T(2,128)(2,1)S(1)} %all-to-all-done) | data formatting | bytes 163840
  76.1 2.0 copy.413
  78.1 0.3 convolution_bitcast_fusion
  78.3 0.2 copy.414
  78.6 0.4 reshape.625
  79.0 0.4 fusion.101
  79.4 0.1 pad_maximum_fusion.31
  79.5 0.1 copy.416
  79.6 0.7 maximum_multiply_fusion
  80.4 116.1 %all-reduce.2.cloned.1.call-done = f32[128,128]{0,1:T(8,128)} async-done(((f32[128,128]{0,1:T(8,128)}), f32[128,128]{0,1:T(8,128)}) %all-reduce.2.cloned.1.call-update) | async-done | bytes 65552 | tf_op jit(solution)/shard_map/psum | solution.py:108
  196.5 0.9 copy.417
  197.4 0.9 fusion.5
  198.3 11.7 %cholesky.18 = f32[128,128]{1,0:T(8,128)S(1)} custom-call(f32[128,128]{1,0:T(8,128)S(1)} %fusion.5), custom_call_target="Cholesky" | custom-call | tf_op jit(solution)/shard_map/jit(cholesky)/cholesky | solution.py:109
  210.0 0.6 compare_reduce_fusion
  210.7 0.7 select_bitcast_fusion
  211.3 0.7 copy.419
  (102 shorter events, 2.0 us)
Async XLA Ops:
  7.9 9.1 %collective-permute-start.1 = (bf16[5,1,8,256]{3,2,1,0:T(8,128)(2,1)S(1)}, bf16[5,1,8,256]{3,2,1,0:T(8,128)(2,1)S(1)}, u32[]{:S(2)}, u32[]{:S(2)}) collective-permute-start(bf16[5,1,8,256]{3,2,1,0:T(8,128)(2,1)S(1)} %convert_element_type.30), channel_id=1, source_target_pairs={{4,0},{8,4},{12,8},{16,12},{20,16},{24,20},{28,24},{0,28},{5,1},{9... | collective-permute-start | bytes 61448 | tf_op jit(solution)/shard_map/ppermute | solution.py:23
  12.4 5.0 %collective-permute-start = (bf16[5,1,8,256]{3,2,1,0:T(8,128)(2,1)S(1)}, bf16[5,1,8,256]{3,2,1,0:T(8,128)(2,1)S(1)}, u32[]{:S(2)}, u32[]{:S(2)}) collective-permute-start(bf16[5,1,8,256]{3,2,1,0:T(8,128)(2,1)S(1)} %convert_element_type.30), channel_id=1, source_target_pairs={{0,4},{4,8},{8,12},{12,16},{16,20},{20,24},{24,28},{28,0},{1,5},{5... | collective-permute-start | bytes 61448 | tf_op jit(solution)/shard_map/ppermute | solution.py:20
  13.1 24.7 %copy-start = (f32[5,1,8,256]{3,2,1,0:T(8,128)S(1)}, f32[5,1,8,256]{3,2,1,0:T(8,128)}, u32[]{:S(2)}) copy-start(f32[5,1,8,256]{3,2,1,0:T(8,128)} %param.2) | copy-start | bytes 122884
  17.5 3.9 %collective-permute-start.3 = (bf16[5,3,1,256]{3,1,2,0:T(4,128)(2,1)S(1)}, bf16[5,3,1,256]{3,1,2,0:T(4,128)(2,1)S(1)}, u32[]{:S(2)}, u32[]{:S(2)}) collective-permute-start(bf16[5,3,1,256]{3,1,2,0:T(4,128)(2,1)S(1)} %copy.422), channel_id=1, source_target_pairs={{1,0},{2,1},{3,2},{0,3},{5,4},{6,5},{7,6},{4,7},{9,8},{10,9},{11,1... | collective-permute-start | bytes 23048 | tf_op jit(solution)/shard_map/ppermute | solution.py:23
  20.0 4.6 %collective-permute-start.2 = (bf16[5,3,1,256]{3,1,2,0:T(4,128)(2,1)S(1)}, bf16[5,3,1,256]{3,1,2,0:T(4,128)(2,1)S(1)}, u32[]{:S(2)}, u32[]{:S(2)}) collective-permute-start(bf16[5,3,1,256]{3,1,2,0:T(4,128)(2,1)S(1)} %copy.421), channel_id=1, source_target_pairs={{0,1},{1,2},{2,3},{3,0},{4,5},{5,6},{6,7},{7,4},{8,9},{9,10},{10,1... | collective-permute-start | bytes 23048 | tf_op jit(solution)/shard_map/ppermute | solution.py:20
  25.8 3.3 %collective-permute-start.5 = (bf16[5,1,8,256]{3,2,0,1:T(8,128)(2,1)S(1)}, bf16[5,1,8,256]{3,2,0,1:T(8,128)(2,1)S(1)}, u32[]{:S(2)}, u32[]{:S(2)}) collective-permute-start(bf16[5,1,8,256]{3,2,0,1:T(8,128)(2,1)S(1)} %get-tuple-element.65), channel_id=1, source_target_pairs={{4,0},{8,4},{12,8},{16,12},{20,16},{24,20},{28,24},{0,28},{5,1},{9... | collective-permute-start | bytes 61448 | tf_op jit(solution)/shard_map/ppermute | solution.py:23
  27.6 5.0 %collective-permute-start.4 = (bf16[5,1,8,256]{3,2,0,1:T(8,128)(2,1)S(1)}, bf16[5,1,8,256]{3,2,0,1:T(8,128)(2,1)S(1)}, u32[]{:S(2)}, u32[]{:S(2)}) collective-permute-start(bf16[5,1,8,256]{3,2,0,1:T(8,128)(2,1)S(1)} %get-tuple-element.65), channel_id=1, source_target_pairs={{0,4},{4,8},{8,12},{12,16},{16,20},{20,24},{24,28},{28,0},{1,5},{5... | collective-permute-start | bytes 61448 | tf_op jit(solution)/shard_map/ppermute | solution.py:20
  32.6 3.7 %collective-permute-start.7 = (bf16[5,3,1,256]{3,1,2,0:T(4,128)(2,1)S(1)}, bf16[5,3,1,256]{3,1,2,0:T(4,128)(2,1)S(1)}, u32[]{:S(2)}, u32[]{:S(2)}) collective-permute-start(bf16[5,3,1,256]{3,1,2,0:T(4,128)(2,1)S(1)} %copy.379), channel_id=1, source_target_pairs={{1,0},{2,1},{3,2},{0,3},{5,4},{6,5},{7,6},{4,7},{9,8},{10,9},{11,1... | collective-permute-start | bytes 23048 | tf_op jit(solution)/shard_map/ppermute | solution.py:23
  33.0 4.6 %collective-permute-start.6 = (bf16[5,3,1,256]{3,1,2,0:T(4,128)(2,1)S(1)}, bf16[5,3,1,256]{3,1,2,0:T(4,128)(2,1)S(1)}, u32[]{:S(2)}, u32[]{:S(2)}) collective-permute-start(bf16[5,3,1,256]{3,1,2,0:T(4,128)(2,1)S(1)} %copy.378), channel_id=1, source_target_pairs={{0,1},{1,2},{2,3},{3,0},{4,5},{5,6},{6,7},{7,4},{8,9},{9,10},{10,1... | collective-permute-start | bytes 23048 | tf_op jit(solution)/shard_map/ppermute | solution.py:20
  38.2 1.5 collective-permute-start.9
  38.2 5.1 %collective-permute-start.8 = (bf16[5,1,8,256]{3,2,0,1:T(8,128)(2,1)S(1)}, bf16[5,1,8,256]{3,2,0,1:T(8,128)(2,1)S(1)}, u32[]{:S(2)}, u32[]{:S(2)}) collective-permute-start(bf16[5,1,8,256]{3,2,0,1:T(8,128)(2,1)S(1)} %fusion.77), channel_id=1, source_target_pairs={{0,4},{4,8},{8,12},{12,16},{16,20},{20,24},{24,28},{28,0},{1,5},{5... | collective-permute-start | bytes 61448 | tf_op jit(solution)/shard_map/ppermute | solution.py:20
  43.3 3.7 %collective-permute-start.11 = (bf16[5,3,1,256]{3,1,2,0:T(4,128)(2,1)S(1)}, bf16[5,3,1,256]{3,1,2,0:T(4,128)(2,1)S(1)}, u32[]{:S(2)}, u32[]{:S(2)}) collective-permute-start(bf16[5,3,1,256]{3,1,2,0:T(4,128)(2,1)S(1)} %copy.391), channel_id=1, source_target_pairs={{1,0},{2,1},{3,2},{0,3},{5,4},{6,5},{7,6},{4,7},{9,8},{10,9},{11,1... | collective-permute-start | bytes 23048 | tf_op jit(solution)/shard_map/ppermute | solution.py:23
  44.1 4.6 %collective-permute-start.10 = (bf16[5,3,1,256]{3,1,2,0:T(4,128)(2,1)S(1)}, bf16[5,3,1,256]{3,1,2,0:T(4,128)(2,1)S(1)}, u32[]{:S(2)}, u32[]{:S(2)}) collective-permute-start(bf16[5,3,1,256]{3,1,2,0:T(4,128)(2,1)S(1)} %copy.390), channel_id=1, source_target_pairs={{0,1},{1,2},{2,3},{3,0},{4,5},{5,6},{6,7},{7,4},{8,9},{9,10},{10,1... | collective-permute-start | bytes 23048 | tf_op jit(solution)/shard_map/ppermute | solution.py:20
  49.1 1.5 collective-permute-start.13
  49.2 5.1 %collective-permute-start.12 = (bf16[5,1,8,256]{3,2,0,1:T(8,128)(2,1)S(1)}, bf16[5,1,8,256]{3,2,0,1:T(8,128)(2,1)S(1)}, u32[]{:S(2)}, u32[]{:S(2)}) collective-permute-start(bf16[5,1,8,256]{3,2,0,1:T(8,128)(2,1)S(1)} %get-tuple-element.31), channel_id=1, source_target_pairs={{0,4},{4,8},{8,12},{12,16},{16,20},{20,24},{24,28},{28,0},{1,5},{5... | collective-permute-start | bytes 61448 | tf_op jit(solution)/shard_map/ppermute | solution.py:20
  54.3 3.7 %collective-permute-start.15 = (bf16[5,3,1,256]{3,1,2,0:T(4,128)(2,1)S(1)}, bf16[5,3,1,256]{3,1,2,0:T(4,128)(2,1)S(1)}, u32[]{:S(2)}, u32[]{:S(2)}) collective-permute-start(bf16[5,3,1,256]{3,1,2,0:T(4,128)(2,1)S(1)} %copy.402), channel_id=1, source_target_pairs={{1,0},{2,1},{3,2},{0,3},{5,4},{6,5},{7,6},{4,7},{9,8},{10,9},{11,1... | collective-permute-start | bytes 23048 | tf_op jit(solution)/shard_map/ppermute | solution.py:23
  54.8 4.6 %collective-permute-start.14 = (bf16[5,3,1,256]{3,1,2,0:T(4,128)(2,1)S(1)}, bf16[5,3,1,256]{3,1,2,0:T(4,128)(2,1)S(1)}, u32[]{:S(2)}, u32[]{:S(2)}) collective-permute-start(bf16[5,3,1,256]{3,1,2,0:T(4,128)(2,1)S(1)} %copy.401), channel_id=1, source_target_pairs={{0,1},{1,2},{2,3},{3,0},{4,5},{5,6},{6,7},{7,4},{8,9},{9,10},{10,1... | collective-permute-start | bytes 23048 | tf_op jit(solution)/shard_map/ppermute | solution.py:20
  63.2 10.2 %all-to-all-start = ((bf16[4,2,5120]{2,1,0:T(2,128)(2,1)}), bf16[4,2,5120]{2,1,0:T(2,128)(2,1)S(1)}, u32[]{:S(2)}, u32[]{:S(2)}) async-start(bf16[4,2,5120]{2,1,0:T(2,128)(2,1)} %reshape.630), calls=%async_computation | async-start | bytes 163840 | tf_op jit(solution)/shard_map/all_to_all | solution.py:92
  66.5 129.9 %all-reduce.2.cloned.1.call-start = ((), (), s32[]{:S(2)}) async-start(), calls=%async_computation.1 | async-start | bytes 131072 | tf_op jit(solution)/shard_map/psum | solution.py:108
Sparse Core Ops, SparseCore 0:
  80.5 115.9 all-reduce.1
where the time goes:
time: 221 us; the launch traced here: 219 us
  waiting for transfers between devices  143 us (65%)
  other arithmetic  21.4 us (10%)
  starting transfers between devices  19.6 us (9%)
  local copies, waits for them, and re-layouts  16.6 us (8%)
  between operations  14.6 us (7%)
  matrix products  4.1 us (2%)
    psum x1, waiting for transfers between devices, local(): gram_whole = lax.psum(gram_local, ('wide', 'narrow'))  116 us
    ppermute x8, waiting for transfers between devices, extended(): lax.ppermute(lax.slice_in_dim(block, block.shape[dim] - width, None, axis...  18.4 us
    another operation x3, other arithmetic, local(): factor = jnp.linalg.cholesky(gram_whole).T  12.4 us
    ppermute x8, starting transfers between devices, extended(): lax.ppermute(lax.slice_in_dim(block, 0, width, axis=dim), axis, backward)  10.5 us
    unnamed x16, local copies, waits for them, and re-layouts  9.46 us
    ppermute x8, waiting for transfers between devices, extended(): lax.ppermute(lax.slice_in_dim(block, 0, width, axis=dim), axis, backward)  7.97 us
    ppermute x8, starting transfers between devices, extended(): lax.ppermute(lax.slice_in_dim(block, block.shape[dim] - width, None, axis...  5.57 us
  transfers between devices with their start and end apart: 18, of which 16 were waited for; matrix products, arithmetic and copies ran while one was open for 6% of the time, Pallas kernels for 0%

commit v1 on v0

v1 whole, which is shorter than its diff:
```python
import functools

import jax
import jax.numpy as jnp
from jax import lax
from jax.experimental import pallas as pl
from jax.experimental.pallas import tpu as pltpu
from jax.sharding import PartitionSpec as P

STEPS = 2
GAMMA = 1.4
TIME_STEP = 0.25
VISCOSITY = 0.15
LANES = 128
NT = (((1,), (1,)), ((), ()))


def flux_of(state, d):
    density, energy = state[0], state[4]
    momentum = state[1:4]
    inverse = 1.0 / density
    vel = momentum[d] * inverse
    squares = momentum[0] * momentum[0] + momentum[1] * momentum[1] + momentum[2] * momentum[2]
    pressure = (GAMMA - 1.0) * (energy - 0.5 * squares * inverse)
    out = [momentum[d], momentum[0] * vel, momentum[1] * vel, momentum[2] * vel]
    out.append((energy + pressure) * vel)
    out[1 + d] = out[1 + d] + pressure
    return out


def tendency(here, x_low, x_high, y_low, y_high):
    cells_z = here[0].shape[1]
    z_low = [pltpu.roll(c, 1, 1) for c in here]
    z_high = [pltpu.roll(c, cells_z - 1, 1) for c in here]
    total = None
    for d, (low, high) in enumerate(((x_low, x_high), (y_low, y_high), (z_low, z_high))):
        flux_low, flux_high = flux_of(low, d), flux_of(high, d)
        part = [
            -0.5 * (fh - fl) + VISCOSITY * (l + h)
            for fh, fl, l, h in zip(flux_high, flux_low, low, high)
        ]
        total = part if total is None else [a + b for a, b in zip(total, part)]
    return [t - (6.0 * VISCOSITY) * c for t, c in zip(total, here)]


def eliminate(tiles, size):
    row_id = lax.broadcasted_iota(jnp.int32, (8, LANES), 0)
    done = []
    tiles = list(tiles)
    for p in range(size // 8):
        scale = jnp.zeros((8, LANES), jnp.float32)
        for k in range(8):
            j = 8 * p + k
            column = jnp.broadcast_to(tiles[p][:, j : j + 1], (8, LANES))
            pivot = jnp.broadcast_to(column[k : k + 1, :], (8, LANES))
            row = jnp.broadcast_to(tiles[p][k : k + 1, :], (8, LANES))
            row = row / pivot
            scale = jnp.where(row_id == k, pivot, scale)
            tiles[p] = tiles[p] - jnp.where(row_id > k, column, 0.0) * row
            for t in range(p + 1, size // 8):
                tiles[t] = tiles[t] - jnp.broadcast_to(tiles[t][:, j : j + 1], (8, LANES)) * row
        lane = lax.broadcasted_iota(jnp.int32, (8, LANES), 1)
        done.append(jnp.where(lane >= row_id + 8 * p, tiles[p] * lax.rsqrt(scale), 0.0))
    return done


def factor_kernel(gram_ref, out_ref):
    size = gram_ref.shape[0]
    tiles = [gram_ref[8 * t : 8 * t + 8, :] for t in range(size // 8)]
    for t, rows in enumerate(eliminate(tiles, size)):
        out_ref[8 * t : 8 * t + 8, :] = rows


def kernel(
    wide, narrow, fields, modes_hbm, flow, gram_out,
    modes, modes_sem, state, x_halo, y_send, y_halo, halo_send, halo_recv,
    snap_out, snap_in, snap_send, snap_recv,
    gram, scatter, part, share, whole, piece, red_send, red_recv,
    tail, rows8, rows_n, sums8, rows_w, last_send, last_recv,
):
    stages = 2 * STEPS
    comps, cells_y, cells_z = fields.shape
    prior = modes.shape[1]
    columns = gram.shape[0]
    mode_lanes = modes.shape[2]
    y_all = cells_y * narrow
    z_own = cells_z // narrow
    z_group = LANES // y_all
    groups = mode_lanes // LANES
    piece_rows = columns // wide
    keep = columns - 16
    iw, jn = lax.axis_index("wide"), lax.axis_index("narrow")

    def w_peer(d):
        return lax.rem(iw + d, wide)

    def n_peer(d):
        return lax.rem(jn + d, narrow)

    def remote(src, dst, send, recv, device):
        return pltpu.make_async_remote_copy(
            src_ref=src, dst_ref=dst, send_sem=send, recv_sem=recv,
            device_id=device, device_id_type=pl.DeviceIdType.MESH,
        )

    loads = [pltpu.make_async_copy(modes_hbm.at[c], modes.at[c], modes_sem.at[c]) for c in range(comps)]
    for load in loads:
        load.start()

    barrier = pltpu.get_barrier_semaphore()
    for d in range(1, wide):
        pl.semaphore_signal(barrier, inc=1, device_id=(w_peer(d), jn), device_id_type=pl.DeviceIdType.MESH)
    for d in range(1, narrow):
        pl.semaphore_signal(barrier, inc=1, device_id=(iw, n_peer(d)), device_id_type=pl.DeviceIdType.MESH)

    def halo_copies(s):
        right, left = (w_peer(1), jn), (w_peer(wide - 1), jn)
        up, down = (iw, n_peer(1)), (iw, n_peer(narrow - 1))
        return [
            remote(state.at[s], x_halo.at[s, 0], halo_send.at[s, 0], halo_recv.at[s, 0], right),
            remote(state.at[s], x_halo.at[s, 1], halo_send.at[s, 1], halo_recv.at[s, 1], left),
            remote(y_send.at[s, 1], y_halo.at[s, 0], halo_send.at[s, 2], halo_recv.at[s, 2], up),
            remote(y_send.at[s, 0], y_halo.at[s, 1], halo_send.at[s, 3], halo_recv.at[s, 3], down),
        ]

    def put_state(s, values):
        for c in range(comps):
            state[s, c] = values[c]
            y_send[s, 0, c : c + 1, :] = values[c][0:1, :]
            y_send[s, 1, c : c + 1, :] = values[c][cells_y - 1 : cells_y, :]
        for c in range(comps, 8):
            y_send[s, 0, c : c + 1, :] = jnp.zeros((1, cells_z), jnp.float32)
            y_send[s, 1, c : c + 1, :] = jnp.zeros((1, cells_z), jnp.float32)

    current = [fields[c] for c in range(comps)]
    put_state(0, current)
    pl.semaphore_wait(barrier, wide + narrow - 2)

    copies = halo_copies(0)
    for copy in copies:
        copy.start()
    pending = list(copies)

    total = jnp.zeros((columns, columns), jnp.float32)
    for c in range(comps):
        loads[c].wait()
        last = modes[c, keep:prior, :].astype(jnp.float32)
        last = jnp.concatenate([last, jnp.zeros((columns - prior, mode_lanes), jnp.float32)], 0)
        tail[c] = last.astype(jnp.bfloat16)
        x = jnp.concatenate([modes[c, 0:keep, :], tail[c]], 0)
        total = total + lax.dot_general(x, x, NT, preferred_element_type=jnp.float32)
    gram[...] = total
    mine = pl.ds(pl.multiple_of(iw * piece_rows, piece_rows), piece_rows)
    scatter[iw] = gram[mine, :]
    first = []
    for d in range(1, wide):
        peer = w_peer(d)
        theirs = pl.ds(pl.multiple_of(peer * piece_rows, piece_rows), piece_rows)
        first.append(remote(gram.at[theirs], scatter.at[iw], red_send.at[0, d], red_recv.at[0, iw], (peer, jn)))
    for copy in first:
        copy.start()
    pending += first

    def reduce_step(s):
        started = []
        if s == 1:
            for d in range(1, wide):
                peer = w_peer(d)
                remote(gram.at[mine], scatter.at[peer], red_send.at[0, d], red_recv.at[0, peer], (peer, jn)).wait_recv()
            acc = scatter[0]
            for w in range(1, wide):
                acc = acc + scatter[w]
            part[...] = acc
            share[jn] = acc
            for d in range(1, narrow):
                started.append(remote(part, share.at[jn], red_send.at[1, d], red_recv.at[1, jn], (iw, n_peer(d))))
        elif s == 2:
            for d in range(1, narrow):
                peer = n_peer(d)
                remote(part, share.at[peer], red_send.at[1, d], red_recv.at[1, peer], (iw, peer)).wait_recv()
            acc = share[0]
            for n in range(1, narrow):
                acc = acc + share[n]
            piece[...] = acc
            whole[iw] = acc
            for d in range(1, wide):
                started.append(remote(piece, whole.at[iw], red_send.at[2, d], red_recv.at[2, iw], (w_peer(d), jn)))
        elif s == 3:
            for d in range(1, wide):
                peer = w_peer(d)
                remote(piece, whole.at[peer], red_send.at[2, d], red_recv.at[2, peer], (peer, jn)).wait_recv()
        for copy in started:
            copy.start()
        return started

    def send_snapshot(s, values):
        stacked = jnp.concatenate(values + [jnp.zeros((snap_out.shape[2] - comps * cells_y, cells_z), jnp.float32)], 0)
        stacked = stacked.astype(jnp.bfloat16)
        for b in range(cells_z // LANES):
            snap_out[s, b] = stacked[:, b * LANES : (b + 1) * LANES]
        snap_in[s, jn] = snap_out[s, (jn * z_own) // LANES]
        started = []
        for d in range(1, narrow):
            peer = n_peer(d)
            started.append(
                remote(snap_out.at[s, (peer * z_own) // LANES], snap_in.at[s, jn],
                       snap_send.at[s, d], snap_recv.at[s, jn], (iw, peer))
            )
        for copy in started:
            copy.start()
        return started

    row = lax.broadcasted_iota(jnp.int32, (cells_y, cells_z), 0)
    base = current
    for s in range(stages):
        for copy in copies:
            copy.wait_recv()
        x_low = [x_halo[s, 0, c] for c in range(comps)]
        x_high = [x_halo[s, 1, c] for c in range(comps)]
        y_low, y_high = [], []
        for c in range(comps):
            low = jnp.broadcast_to(y_halo[s, 0, c : c + 1, :], (cells_y, cells_z))
            high = jnp.broadcast_to(y_halo[s, 1, c : c + 1, :], (cells_y, cells_z))
            y_low.append(jnp.where(row == 0, low, pltpu.roll(current[c], 1, 0)))
            y_high.append(jnp.where(row == cells_y - 1, high, pltpu.roll(current[c], cells_y - 1, 0)))
        change = tendency(current, x_low, x_high, y_low, y_high)
        moved = [a + TIME_STEP * b for a, b in zip(current, change)]
        if s % 2 == 1:
            moved = [0.5 * a + 0.5 * b for a, b in zip(base, moved)]
            base = moved
        current = moved
        if s + 1 < stages:
            put_state(s + 1, current)
            copies = halo_copies(s + 1)
            for copy in copies:
                copy.start()
            pending += copies
        pending += send_snapshot(s, current)
        pending += reduce_step(s + 1)
    for c in range(comps):
        flow[c] = current[c]

    offset = lax.rem(jn * z_own, LANES)
    spread = (
        lax.rem(lax.broadcasted_iota(jnp.int32, (LANES, y_all), 0), y_all)
        == lax.broadcasted_iota(jnp.int32, (LANES, y_all), 1)
    ).astype(jnp.bfloat16)
    z_id = lax.broadcasted_iota(jnp.int32, (LANES, LANES), 1) - offset
    k_id = lax.broadcasted_iota(jnp.int32, (LANES, LANES), 0) // y_all
    fits = lax.rem(z_id + LANES, z_group) == k_id
    pick_row = lax.broadcasted_iota(jnp.int32, (16 * groups, LANES), 0)
    pick_z = lax.broadcasted_iota(jnp.int32, (16 * groups, LANES), 1) - offset
    inside = (pick_z >= 0) & (pick_z // z_group == pick_row // 16)
    acc = [jnp.zeros((16 * groups, LANES), jnp.float32) for _ in range(comps)]
    for s in range(stages):
        for d in range(1, narrow):
            peer = n_peer(d)
            remote(snap_out.at[s, 0], snap_in.at[s, peer], snap_send.at[s, d], snap_recv.at[s, peer], (iw, peer)).wait_recv()
        arrived = [snap_in[s, n].astype(jnp.float32) for n in range(narrow)]
        pick = (inside & (lax.rem(pick_row, 16) == 16 - stages + s)).astype(jnp.bfloat16)
        for c in range(comps):
            cells = jnp.concatenate([a[c * cells_y : (c + 1) * cells_y, :] for a in arrived], 0)
            wide_cells = jnp.dot(spread, cells.astype(jnp.bfloat16), preferred_element_type=jnp.float32)
            chosen = jnp.where(fits, wide_cells, 0.0).astype(jnp.bfloat16)
            acc[c] = acc[c] + lax.dot_general(pick, chosen, NT, preferred_element_type=jnp.float32)
    total = jnp.zeros((16, columns), jnp.float32)
    for c in range(comps):
        flat = jnp.concatenate([acc[c][16 * g : 16 * g + 16, :] for g in range(groups)], 1)
        rows = (tail[c].astype(jnp.float32) + flat).astype(jnp.bfloat16)
        x = jnp.concatenate([modes[c, 0:keep, :], rows], 0)
        total = total + lax.dot_general(rows, x, NT, preferred_element_type=jnp.float32)
    mine8 = total[8:16, :]
    rows8[...] = mine8
    rows_n[jn] = mine8
    started = [
        remote(rows8, rows_n.at[jn], last_send.at[0, d], last_recv.at[0, jn], (iw, n_peer(d)))
        for d in range(1, narrow)
    ]
    for copy in started:
        copy.start()
    pending += started
    for d in range(1, narrow):
        peer = n_peer(d)
        remote(rows8, rows_n.at[peer], last_send.at[0, d], last_recv.at[0, peer], (iw, peer)).wait_recv()
    sum8 = rows_n[0]
    for n in range(1, narrow):
        sum8 = sum8 + rows_n[n]
    sums8[...] = sum8
    rows_w[iw] = sum8
    started = [
        remote(sums8, rows_w.at[iw], last_send.at[1, d], last_recv.at[1, iw], (w_peer(d), jn))
        for d in range(1, wide)
    ]
    for copy in started:
        copy.start()
    pending += started
    for d in range(1, wide):
        peer = w_peer(d)
        remote(sums8, rows_w.at[peer], last_send.at[1, d], last_recv.at[1, peer], (peer, jn)).wait_recv()
    sum8 = rows_w[0]
    for w in range(1, wide):
        sum8 = sum8 + rows_w[w]
    for copy in pending:
        copy.wait_send()

    inverse_cells = 1.0 / (wide * narrow * cells_y * cells_z)
    old = jnp.concatenate([whole[w] for w in range(wide)], 0)
    bottom = jnp.concatenate([jnp.zeros((columns - 8, columns), jnp.float32), sum8], 0)
    side = jnp.transpose(bottom)
    row = lax.broadcasted_iota(jnp.int32, (columns, columns), 0)
    col = lax.broadcasted_iota(jnp.int32, (columns, columns), 1)
    full = jnp.where(row >= prior, bottom, jnp.where(col >= prior, side, old))
    gram_out[...] = full * inverse_cells


def local(wide, narrow, fields, prior_modes):
    comps, cells_x, cells_y, cells_z = fields.shape
    prior = prior_modes.shape[0]
    stages = 2 * STEPS
    columns = prior + stages
    modes = jnp.transpose(prior_modes, (1, 2, 0, 3)).reshape(comps, prior, prior_modes.shape[3])
    piece = columns // wide
    snap_rows = -(-comps * cells_y // 16) * 16
    f32, bf16 = jnp.float32, jnp.bfloat16
    vmem = pl.BlockSpec(memory_space=pltpu.VMEM)
    dma = pltpu.SemaphoreType.DMA
    flow, gram = pl.pallas_call(
        functools.partial(kernel, wide, narrow),
        out_shape=(
            jax.ShapeDtypeStruct((comps, cells_y, cells_z), f32),
            jax.ShapeDtypeStruct((columns, columns), f32),
        ),
        in_specs=[vmem, pl.BlockSpec(memory_space=pl.ANY)],
        out_specs=(vmem, vmem),
        scratch_shapes=[
            pltpu.VMEM(modes.shape, bf16), dma((comps,)),
            pltpu.VMEM((stages, comps, cells_y, cells_z), f32),
            pltpu.VMEM((stages, 2, comps, cells_y, cells_z), f32),
            pltpu.VMEM((stages, 2, 8, cells_z), f32),
            pltpu.VMEM((stages, 2, 8, cells_z), f32),
            dma((stages, 4)), dma((stages, 4)),
            pltpu.VMEM((stages, cells_z // LANES, snap_rows, LANES), bf16),
            pltpu.VMEM((stages, narrow, snap_rows, LANES), bf16),
            dma((stages, narrow)), dma((stages, narrow)),
            pltpu.VMEM((columns, columns), f32),
            pltpu.VMEM((wide, piece, columns), f32),
            pltpu.VMEM((piece, columns), f32),
            pltpu.VMEM((narrow, piece, columns), f32),
            pltpu.VMEM((wide, piece, columns), f32),
            pltpu.VMEM((piece, columns), f32),
            dma((3, max(wide, narrow))), dma((3, max(wide, narrow))),
            pltpu.VMEM((comps, 16, modes.shape[2]), bf16),
            pltpu.VMEM((8, columns), f32),
            pltpu.VMEM((narrow, 8, columns), f32),
            pltpu.VMEM((8, columns), f32),
            pltpu.VMEM((wide, 8, columns), f32),
            dma((2, max(wide, narrow))), dma((2, max(wide, narrow))),
        ],
        compiler_params=pltpu.CompilerParams(
            collective_id=0, has_side_effects=True, vmem_limit_bytes=24 * 1024 * 1024
        ),
    )(fields.reshape(comps, cells_y, cells_z), modes)
    factor = pl.pallas_call(
        factor_kernel,
        out_shape=jax.ShapeDtypeStruct((columns, columns), f32),
        in_specs=[vmem],
        out_specs=vmem,
    )(gram)
    return flow.reshape(fields.shape), factor


def solution(mesh):
    wide, narrow = mesh.shape["wide"], mesh.shape["narrow"]
    return jax.shard_map(
        functools.partial(local, wide, narrow),
        mesh=mesh,
        in_specs=(P(None, "wide", "narrow", None), P(None, None, "wide", "narrow")),
        out_specs=(P(None, "wide", "narrow", None), P()),
        check_vma=False,
    )
```

time: 221 us -> 55.2 us (0.25)
  waiting for transfers between devices: 143 us -> 0 us
  Pallas kernels: 0 us -> 50.5 us
  other arithmetic: 21.4 us -> 0 us
  starting transfers between devices: 19.6 us -> 0 us
  between operations: 14.6 us -> 0.66 us
  local copies, waits for them, and re-layouts: 16.6 us -> 3.74 us
  matrix products: 4.1 us -> 0 us
    psum x1 -> x0, waiting for transfers between devices: 116 us -> none  [local(): gram_whole = lax.psum(gram_local, ('wide', 'narrow'))]
    pallas_call x0 -> x2, Pallas kernels: none -> 50.5 us  [the longest x1 31.9 us: local(): pl.pallas_call(functools.partial(kernel, wide, narrow), out_shape=(jax.Sh...]
    ppermute x16 -> x0, waiting for transfers between devices: 26.4 us -> none  [the longest x8 18.4 us: extended(): lax.ppermute(lax.slice_in_dim(block, block.shape[dim] - width, None, axis...]
    ppermute x16 -> x0, starting transfers between devices: 16.1 us -> none  [the longest x8 10.5 us: extended(): lax.ppermute(lax.slice_in_dim(block, 0, width, axis=dim), axis, backward)]
    another operation x18 -> x0, other arithmetic: 14 us -> none  [the longest x3 12.4 us: local(): factor = jnp.linalg.cholesky(gram_whole).T]
    unnamed x16 -> x7, local copies, waits for them, and re-layouts: 9.46 us -> 3.74 us
    dot_general x3 -> x0, matrix products: 4.1 us -> none  [the longest x1 3.37 us: local(): lax.dot_general(flat_modes, flat_modes, contract, preferred_element_type=...]
    all_to_all x1 -> x0, starting transfers between devices: 3.29 us -> none  [local(): lax.all_to_all(jnp.stack(snapshots), 'narrow', split_axis=4, concat_axis=...]
  transfers between devices with their start and end apart: 18 -> 0, of which waited for: 16 -> 0; matrix products, arithmetic and copies ran while one was open for 6% -> 0% of each run, Pallas kernels for 0% -> 0%
where the time goes in v1:
time: 55.2 us; the launch traced here: 54.9 us
  Pallas kernels  50.5 us (91%)
  local copies, waits for them, and re-layouts  3.74 us (7%)
  between operations  0.66 us (1%)
    pallas_call x1, Pallas kernels, local(): pl.pallas_call(functools.partial(kernel, wide, narrow), out_shape=(jax.Sh...  31.9 us
    pallas_call x1, Pallas kernels, local(): pl.pallas_call(factor_kernel, out_shape=jax.ShapeDtypeStruct((columns, co...  18.6 us
    unnamed x7, local copies, waits for them, and re-layouts  3.74 us

profile of v1, /device:TPU:0, one launch (start us, length us, event | category | flops | bytes accessed | tf_op | source)
XLA Modules:
  0.0 54.9 jit_solution(5001453673714619526)
XLA Ops:
  0.6 0.0 copy-start
  0.6 1.7 %copy-done = bf16[124,5,1,2048]{3,0,2,1:T(8,128)(2,1)S(1)} copy-done((bf16[124,5,1,2048]{3,0,2,1:T(8,128)(2,1)S(1)}, bf16[124,5,1,2048]{3,0,2,1:T(8,128)(2,1)}, u32[]{:S(2)}) %copy-start) | copy-done | bytes 2539544
  2.4 0.0 copy-start.2
  2.4 0.8 %copy-done.2 = f32[5,1,8,256]{3,2,1,0:T(8,128)S(1)} copy-done((f32[5,1,8,256]{3,2,1,0:T(8,128)S(1)}, f32[5,1,8,256]{3,2,1,0:T(8,128)}, u32[]{:S(2)}) %copy-start.2) | copy-done | bytes 40984
  3.1 31.9 %shard_map.41 = (f32[5,8,256]{2,1,0:T(8,128)S(1)}, f32[128,128]{1,0:T(8,128)S(1)}) custom-call(f32[5,8,256]{2,1,0:T(8,128)S(1)} %bitcast.11, bf16[5,124,2048]{2,1,0:T(8,128)(2,1)S(1)} %bitcast.9), custom_call_target="tpu_custom_call" | custom-call | tf_op jit(solution)/shard_map/pallas_call | solution.py:327
  35.1 0.0 copy-start.1
  35.1 0.6 %copy-done.1 = f32[128,128]{1,0:T(8,128)} copy-done((f32[128,128]{1,0:T(8,128)}, f32[128,128]{1,0:T(8,128)S(1)}, u32[]{:S(2)}) %copy-start.1) | copy-done | bytes 65560
  35.7 18.6 %shard_map.42 = f32[128,128]{1,0:T(8,128)} custom-call(f32[128,128]{1,0:T(8,128)} %copy-done.1), custom_call_target="tpu_custom_call" | custom-call | tf_op jit(solution)/shard_map/pallas_call | solution.py:363
  54.3 0.6 %copy.7 = f32[5,1,8,256]{3,2,1,0:T(8,128)} copy(f32[5,1,8,256]{3,2,1,0:T(8,128)S(1)} %bitcast.10) | data formatting | bytes 81920
Async XLA Ops:
  0.6 1.7 %copy-start = (bf16[124,5,1,2048]{3,0,2,1:T(8,128)(2,1)S(1)}, bf16[124,5,1,2048]{3,0,2,1:T(8,128)(2,1)}, u32[]{:S(2)}) copy-start(bf16[124,5,1,2048]{3,0,2,1:T(8,128)(2,1)} %param.3) | copy-start | bytes 7618564
  2.4 0.8 %copy-start.2 = (f32[5,1,8,256]{3,2,1,0:T(8,128)S(1)}, f32[5,1,8,256]{3,2,1,0:T(8,128)}, u32[]{:S(2)}) copy-start(f32[5,1,8,256]{3,2,1,0:T(8,128)} %param.2) | copy-start | bytes 122884
  35.1 0.6 %copy-start.1 = (f32[128,128]{1,0:T(8,128)}, f32[128,128]{1,0:T(8,128)S(1)}, u32[]{:S(2)}) copy-start(f32[128,128]{1,0:T(8,128)S(1)} %get-tuple-element.5.gram_ref) | copy-start | bytes 196612

commit v2 on v1

--- a/solution.py
+++ b/solution.py
@@ -43,37 +43,66 @@
     return [t - (6.0 * VISCOSITY) * c for t, c in zip(total, here)]
 
 
-def eliminate(tiles, size):
-    row_id = lax.broadcasted_iota(jnp.int32, (8, LANES), 0)
-    done = []
-    tiles = list(tiles)
-    for p in range(size // 8):
-        scale = jnp.zeros((8, LANES), jnp.float32)
-        for k in range(8):
-            j = 8 * p + k
-            column = jnp.broadcast_to(tiles[p][:, j : j + 1], (8, LANES))
-            pivot = jnp.broadcast_to(column[k : k + 1, :], (8, LANES))
-            row = jnp.broadcast_to(tiles[p][k : k + 1, :], (8, LANES))
-            row = row / pivot
-            scale = jnp.where(row_id == k, pivot, scale)
-            tiles[p] = tiles[p] - jnp.where(row_id > k, column, 0.0) * row
-            for t in range(p + 1, size // 8):
-                tiles[t] = tiles[t] - jnp.broadcast_to(tiles[t][:, j : j + 1], (8, LANES)) * row
-        lane = lax.broadcasted_iota(jnp.int32, (8, LANES), 1)
-        done.append(jnp.where(lane >= row_id + 8 * p, tiles[p] * lax.rsqrt(scale), 0.0))
-    return done
-
-
-def factor_kernel(gram_ref, out_ref):
-    size = gram_ref.shape[0]
-    tiles = [gram_ref[8 * t : 8 * t + 8, :] for t in range(size // 8)]
-    for t, rows in enumerate(eliminate(tiles, size)):
-        out_ref[8 * t : 8 * t + 8, :] = rows
+def lane_ids():
+    return lax.broadcasted_iota(jnp.int32, (8, LANES), 1)
+
+
+def row_ids():
+    return lax.broadcasted_iota(jnp.int32, (8, LANES), 0)
+
+
+def column_of(tile, j):
+    return jnp.broadcast_to(tile[:, j : j + 1], (8, LANES))
+
+
+def row_of(tile, k):
+    return jnp.broadcast_to(tile[k : k + 1, :], (8, LANES))
+
+
+def inverted(x):
+    guess = pl.reciprocal(x, approx=True)
+    guess = guess * (2.0 - x * guess)
+    return guess * (2.0 - x * guess)
+
+
+def eliminate_panel(tiles, p, first, last):
+    lane, row = lane_ids(), row_ids()
+    pivots = jnp.zeros((8, LANES), jnp.float32)
+    steps = range(first, last)
+    panel = tiles[p]
+    columns = {k: column_of(panel, 8 * p + k) for k in steps}
+    heads, inverses, crossings = {}, {}, {}
+    for k in steps:
+        j = 8 * p + k
+        pivot = row_of(columns[k], k)
+        inverses[k] = inverted(pivot)
+        pivots = jnp.where(row == k, pivot, pivots)
+        factor = jnp.where(row > k, columns[k], 0.0) * inverses[k]
+        for m in steps:
+            if m > k:
+                crossings[k, m] = row_of(columns[m], k)
+                columns[m] = columns[m] - factor * crossings[k, m]
+        heads[k] = jnp.where(lane == j, 1.0, row_of(panel, k))
+        panel = jnp.where((lane == j) & (row > k), 0.0, panel) - factor * heads[k]
+    tiles[p] = panel
+    cleared = (lane >= 8 * p + first) & (lane < 8 * p + last)
+    for t in range(p + 1, len(tiles)):
+        columns = {k: column_of(tiles[t], 8 * p + k) for k in steps}
+        rest = jnp.where(cleared, 0.0, tiles[t])
+        for k in steps:
+            factor = columns[k] * inverses[k]
+            for m in steps:
+                if m > k:
+                    columns[m] = columns[m] - factor * crossings[k, m]
+            outside = jnp.where((lane > 8 * p + k) & cleared, 0.0, heads[k])
+            rest = rest - factor * outside
+        tiles[t] = rest
+    return pivots
 
 
 def kernel(
-    wide, narrow, fields, modes_hbm, flow, gram_out,
-    modes, modes_sem, state, x_halo, y_send, y_halo, halo_send, halo_recv,
+    wide, narrow, fields, modes_hbm, flow, factor_out,
+    modes, modes_sem, fields_sem, state, x_halo, y_send, y_halo, halo_send, halo_recv,
     snap_out, snap_in, snap_send, snap_recv,
     gram, scatter, part, share, whole, piece, red_send, red_recv,
     tail, rows8, rows_n, sums8, rows_w, last_send, last_recv,
@@ -104,6 +133,8 @@
         )
 
     loads = [pltpu.make_async_copy(modes_hbm.at[c], modes.at[c], modes_sem.at[c]) for c in range(comps)]
+    fields_load = pltpu.make_async_copy(fields, state.at[0], fields_sem.at[0])
+    fields_load.start()
     for load in loads:
         load.start()
 
@@ -125,14 +156,16 @@
 
     def put_state(s, values):
         for c in range(comps):
-            state[s, c] = values[c]
+            if s > 0:
+                state[s, c] = values[c]
             y_send[s, 0, c : c + 1, :] = values[c][0:1, :]
             y_send[s, 1, c : c + 1, :] = values[c][cells_y - 1 : cells_y, :]
         for c in range(comps, 8):
             y_send[s, 0, c : c + 1, :] = jnp.zeros((1, cells_z), jnp.float32)
             y_send[s, 1, c : c + 1, :] = jnp.zeros((1, cells_z), jnp.float32)
 
-    current = [fields[c] for c in range(comps)]
+    fields_load.wait()
+    current = [state[0, c] for c in range(comps)]
     put_state(0, current)
     pl.semaphore_wait(barrier, wide + narrow - 2)
 
@@ -210,6 +243,43 @@
             copy.start()
         return started
 
+    offset = lax.rem(jn * z_own, LANES)
+    spread = (
+        lax.rem(lax.broadcasted_iota(jnp.int32, (LANES, y_all), 0), y_all)
+        == lax.broadcasted_iota(jnp.int32, (LANES, y_all), 1)
+    ).astype(jnp.bfloat16)
+    z_id = lax.broadcasted_iota(jnp.int32, (LANES, LANES), 1) - offset
+    k_id = lax.broadcasted_iota(jnp.int32, (LANES, LANES), 0) // y_all
+    fits = lax.rem(z_id + LANES, z_group) == k_id
+    pick_row = lax.broadcasted_iota(jnp.int32, (16 * groups, LANES), 0)
+    pick_z = lax.broadcasted_iota(jnp.int32, (16 * groups, LANES), 1) - offset
+    inside = (pick_z >= 0) & (pick_z // z_group == pick_row // 16)
+    acc = [jnp.zeros((16 * groups, LANES), jnp.float32) for _ in range(comps)]
+
+    def order_snapshot(s):
+        for d in range(1, narrow):
+            peer = n_peer(d)
+            remote(snap_out.at[s, 0], snap_in.at[s, peer], snap_send.at[s, d], snap_recv.at[s, peer], (iw, peer)).wait_recv()
+        arrived = [snap_in[s, n].astype(jnp.float32) for n in range(narrow)]
+        pick = (inside & (lax.rem(pick_row, 16) == 16 - stages + s)).astype(jnp.bfloat16)
+        for c in range(comps):
+            cells = jnp.concatenate([a[c * cells_y : (c + 1) * cells_y, :] for a in arrived], 0)
+            wide_cells = jnp.dot(spread, cells.astype(jnp.bfloat16), preferred_element_type=jnp.float32)
+            chosen = jnp.where(fits, wide_cells, 0.0).astype(jnp.bfloat16)
+            acc[c] = acc[c] + lax.dot_general(pick, chosen, NT, preferred_element_type=jnp.float32)
+
+    tiles, pivots = [], []
+    inverse_cells = 1.0 / (wide * narrow * cells_y * cells_z)
+
+    def begin():
+        for t in range(columns // 8):
+            rows = whole[(8 * t) // piece_rows, (8 * t) % piece_rows : (8 * t) % piece_rows + 8, :]
+            tiles.append(rows * inverse_cells)
+
+    def run(start, stop):
+        for p in range(start, stop):
+            pivots.append(eliminate_panel(tiles, p, 0, min(8, prior - 8 * p)))
+
     row = lax.broadcasted_iota(jnp.int32, (cells_y, cells_z), 0)
     base = current
     for s in range(stages):
@@ -237,32 +307,16 @@
             pending += copies
         pending += send_snapshot(s, current)
         pending += reduce_step(s + 1)
+        if s > 0:
+            order_snapshot(s - 1)
+        if s == stages - 2:
+            begin()
+            run(0, 4)
     for c in range(comps):
         flow[c] = current[c]
 
-    offset = lax.rem(jn * z_own, LANES)
-    spread = (
-        lax.rem(lax.broadcasted_iota(jnp.int32, (LANES, y_all), 0), y_all)
-        == lax.broadcasted_iota(jnp.int32, (LANES, y_all), 1)
-    ).astype(jnp.bfloat16)
-    z_id = lax.broadcasted_iota(jnp.int32, (LANES, LANES), 1) - offset
-    k_id = lax.broadcasted_iota(jnp.int32, (LANES, LANES), 0) // y_all
-    fits = lax.rem(z_id + LANES, z_group) == k_id
-    pick_row = lax.broadcasted_iota(jnp.int32, (16 * groups, LANES), 0)
-    pick_z = lax.broadcasted_iota(jnp.int32, (16 * groups, LANES), 1) - offset
-    inside = (pick_z >= 0) & (pick_z // z_group == pick_row // 16)
-    acc = [jnp.zeros((16 * groups, LANES), jnp.float32) for _ in range(comps)]
-    for s in range(stages):
-        for d in range(1, narrow):
-            peer = n_peer(d)
-            remote(snap_out.at[s, 0], snap_in.at[s, peer], snap_send.at[s, d], snap_recv.at[s, peer], (iw, peer)).wait_recv()
-        arrived = [snap_in[s, n].astype(jnp.float32) for n in range(narrow)]
-        pick = (inside & (lax.rem(pick_row, 16) == 16 - stages + s)).astype(jnp.bfloat16)
-        for c in range(comps):
-            cells = jnp.concatenate([a[c * cells_y : (c + 1) * cells_y, :] for a in arrived], 0)
-            wide_cells = jnp.dot(spread, cells.astype(jnp.bfloat16), preferred_element_type=jnp.float32)
-            chosen = jnp.where(fits, wide_cells, 0.0).astype(jnp.bfloat16)
-            acc[c] = acc[c] + lax.dot_general(pick, chosen, NT, preferred_element_type=jnp.float32)
+    run(4, 8)
+    order_snapshot(stages - 1)
     total = jnp.zeros((16, columns), jnp.float32)
     for c in range(comps):
         flat = jnp.concatenate([acc[c][16 * g : 16 * g + 16, :] for g in range(groups)], 1)
@@ -279,6 +333,7 @@
     for copy in started:
         copy.start()
     pending += started
+    run(8, 12)
     for d in range(1, narrow):
         peer = n_peer(d)
         remote(rows8, rows_n.at[peer], last_send.at[0, d], last_recv.at[0, peer], (iw, peer)).wait_recv()
@@ -294,23 +349,43 @@
     for copy in started:
         copy.start()
     pending += started
+    run(12, columns // 8)
+    lane, row = lane_ids(), row_ids()
+    uppers, inverse = [], []
+    for t in range(columns // 8):
+        scale = lax.rsqrt(jnp.where(pivots[t] > 0.0, pivots[t], 1.0))
+        scale = jnp.where(row + 8 * t < prior, scale, 0.0)
+        uppers.append(jnp.where(lane >= row + 8 * t, tiles[t], 0.0) * scale)
+        left = jnp.where(lane < row + 8 * t, tiles[t], 0.0)
+        inverse.append(jnp.where(lane == row + 8 * t, 1.0, left) * scale)
+    inverse = jnp.concatenate(inverse, 0)
+    for copy in pending:
+        copy.wait_send()
     for d in range(1, wide):
         peer = w_peer(d)
         remote(sums8, rows_w.at[peer], last_send.at[1, d], last_recv.at[1, peer], (peer, jn)).wait_recv()
     sum8 = rows_w[0]
     for w in range(1, wide):
         sum8 = sum8 + rows_w[w]
-    for copy in pending:
-        copy.wait_send()
-
-    inverse_cells = 1.0 / (wide * narrow * cells_y * cells_z)
-    old = jnp.concatenate([whole[w] for w in range(wide)], 0)
-    bottom = jnp.concatenate([jnp.zeros((columns - 8, columns), jnp.float32), sum8], 0)
+
+    exact = lax.Precision.HIGHEST
+    corner = row + columns - 8 >= prior
+    rows = jnp.where(corner, sum8 * inverse_cells, 0.0)
+    known = jnp.where(lane < prior, rows, 0.0)
+    solved = lax.dot_general(known, inverse, NT, precision=exact, preferred_element_type=jnp.float32)
+    bottom = jnp.concatenate([jnp.zeros((columns - 8, columns), jnp.float32), solved], 0)
+    taken = lax.dot_general(solved, bottom, NT, precision=exact, preferred_element_type=jnp.float32)
+    last_tile = [jnp.where(lane >= prior, rows - taken, 0.0)]
+    last_tile = [pltpu.roll(last_tile[0], 8, 1)]
+    left = eliminate_panel(last_tile, 0, prior - (columns - 8), 8)
+    tip = jnp.where(lane >= row, last_tile[0], 0.0) * lax.rsqrt(jnp.where(corner, left, 1.0))
+    tip = pltpu.roll(jnp.where(corner, tip, 0.0), LANES - 8, 1)
     side = jnp.transpose(bottom)
-    row = lax.broadcasted_iota(jnp.int32, (columns, columns), 0)
-    col = lax.broadcasted_iota(jnp.int32, (columns, columns), 1)
-    full = jnp.where(row >= prior, bottom, jnp.where(col >= prior, side, old))
-    gram_out[...] = full * inverse_cells
+    for t in range(columns // 8):
+        out = uppers[t] + side[8 * t : 8 * t + 8, :]
+        if t == columns // 8 - 1:
+            out = jnp.where(corner, tip, out)
+        factor_out[8 * t : 8 * t + 8, :] = out
 
 
 def local(wide, narrow, fields, prior_modes):
@@ -324,16 +399,16 @@
     f32, bf16 = jnp.float32, jnp.bfloat16
     vmem = pl.BlockSpec(memory_space=pltpu.VMEM)
     dma = pltpu.SemaphoreType.DMA
-    flow, gram = pl.pallas_call(
+    flow, factor = pl.pallas_call(
         functools.partial(kernel, wide, narrow),
         out_shape=(
             jax.ShapeDtypeStruct((comps, cells_y, cells_z), f32),
             jax.ShapeDtypeStruct((columns, columns), f32),
         ),
-        in_specs=[vmem, pl.BlockSpec(memory_space=pl.ANY)],
+        in_specs=[pl.BlockSpec(memory_space=pl.ANY)] * 2,
         out_specs=(vmem, vmem),
         scratch_shapes=[
-            pltpu.VMEM(modes.shape, bf16), dma((comps,)),
+            pltpu.VMEM(modes.shape, bf16), dma((comps,)), dma((1,)),
             pltpu.VMEM((stages, comps, cells_y, cells_z), f32),
             pltpu.VMEM((stages, 2, comps, cells_y, cells_z), f32),
             pltpu.VMEM((stages, 2, 8, cells_z), f32),
@@ -357,15 +432,9 @@
             dma((2, max(wide, narrow))), dma((2, max(wide, narrow))),
         ],
         compiler_params=pltpu.CompilerParams(
-            collective_id=0, has_side_effects=True, vmem_limit_bytes=24 * 1024 * 1024
+            collective_id=0, has_side_effects=True, vmem_limit_bytes=60 * 1024 * 1024
         ),
     )(fields.reshape(comps, cells_y, cells_z), modes)
-    factor = pl.pallas_call(
-        factor_kernel,
-        out_shape=jax.ShapeDtypeStruct((columns, columns), f32),
-        in_specs=[vmem],
-        out_specs=vmem,
-    )(gram)
     return flow.reshape(fields.shape), factor
 
 

time: 55.2 us -> 38.4 us (0.70)
  Pallas kernels: 50.5 us -> 34.7 us
  local copies, waits for them, and re-layouts: 3.74 us -> 2.87 us
    pallas_call x1 -> x0, Pallas kernels: 18.6 us -> none  [local(): pl.pallas_call(factor_kernel, out_shape=jax.ShapeDtypeStruct((columns, co...]
    pallas_call x1, Pallas kernels: 31.9 us -> 34.7 us  [local(): pl.pallas_call(functools.partial(kernel, wide, narrow), out_shape=(jax.Sh...]
    unnamed x7 -> x2, local copies, waits for them, and re-layouts: 3.74 us -> 2.87 us
where the time goes in v2:
time: 38.4 us; the launch traced here: 38.2 us
  Pallas kernels  34.7 us (90%)
  local copies, waits for them, and re-layouts  2.87 us (7%)
  between operations  0.64 us (2%)
    pallas_call x1, Pallas kernels, local(): pl.pallas_call(functools.partial(kernel, wide, narrow), out_shape=(jax.Sh...  34.7 us
    unnamed x2, local copies, waits for them, and re-layouts  2.87 us

profile of v2, /device:TPU:0, one launch (start us, length us, event | category | flops | bytes accessed | tf_op | source)
XLA Modules:
  0.0 38.2 jit_solution(6461081934860809292)
XLA Ops:
  0.6 34.7 %shard_map.41 = (f32[5,8,256]{2,1,0:T(8,128)}, f32[128,128]{1,0:T(8,128)}) custom-call(f32[5,8,256]{2,1,0:T(8,128)} %bitcast.11, bf16[5,124,2048]{2,1,0:T(8,128)(2,1)} %bitcast.9), custom_call_target="tpu_custom_call" | custom-call | tf_op jit(solution)/shard_map/pallas_call | solution.py:402
  35.3 1.4 %copy.8 = f32[5,1,8,256]{3,2,1,0:T(8,128)} copy(f32[5,1,8,256]{3,2,1,0:T(8,128)} %bitcast.10) | data formatting | bytes 81920
  36.7 1.5 %copy.9 = f32[128,128]{1,0:T(8,128)} copy(f32[128,128]{1,0:T(8,128)} %get-tuple-element.11) | data formatting | bytes 131072

commit v3 on v2

--- a/solution.py
+++ b/solution.py
@@ -102,8 +102,8 @@
 
 def kernel(
     wide, narrow, fields, modes_hbm, flow, factor_out,
-    modes, modes_sem, fields_sem, state, x_halo, y_send, y_halo, halo_send, halo_recv,
-    snap_out, snap_in, snap_send, snap_recv,
+    modes, modes_sem, start, start_sem, packed, x_halo, y_send, y_halo, halo_send, halo_recv,
+    snap_in, snap_send, snap_recv,
     gram, scatter, part, share, whole, piece, red_send, red_recv,
     tail, rows8, rows_n, sums8, rows_w, last_send, last_recv,
 ):
@@ -133,7 +133,7 @@
         )
 
     loads = [pltpu.make_async_copy(modes_hbm.at[c], modes.at[c], modes_sem.at[c]) for c in range(comps)]
-    fields_load = pltpu.make_async_copy(fields, state.at[0], fields_sem.at[0])
+    fields_load = pltpu.make_async_copy(fields, start, start_sem.at[0])
     fields_load.start()
     for load in loads:
         load.start()
@@ -148,24 +148,34 @@
         right, left = (w_peer(1), jn), (w_peer(wide - 1), jn)
         up, down = (iw, n_peer(1)), (iw, n_peer(narrow - 1))
         return [
-            remote(state.at[s], x_halo.at[s, 0], halo_send.at[s, 0], halo_recv.at[s, 0], right),
-            remote(state.at[s], x_halo.at[s, 1], halo_send.at[s, 1], halo_recv.at[s, 1], left),
+            remote(packed.at[s], x_halo.at[s, 0], halo_send.at[s, 0], halo_recv.at[s, 0], right),
+            remote(packed.at[s], x_halo.at[s, 1], halo_send.at[s, 1], halo_recv.at[s, 1], left),
             remote(y_send.at[s, 1], y_halo.at[s, 0], halo_send.at[s, 2], halo_recv.at[s, 2], up),
             remote(y_send.at[s, 0], y_halo.at[s, 1], halo_send.at[s, 3], halo_recv.at[s, 3], down),
         ]
 
     def put_state(s, values):
-        for c in range(comps):
-            if s > 0:
-                state[s, c] = values[c]
-            y_send[s, 0, c : c + 1, :] = values[c][0:1, :]
-            y_send[s, 1, c : c + 1, :] = values[c][cells_y - 1 : cells_y, :]
-        for c in range(comps, 8):
-            y_send[s, 0, c : c + 1, :] = jnp.zeros((1, cells_z), jnp.float32)
-            y_send[s, 1, c : c + 1, :] = jnp.zeros((1, cells_z), jnp.float32)
+        spare = jnp.zeros((packed.shape[2] - comps * cells_y, cells_z), jnp.float32)
+        stacked = jnp.concatenate(values + [spare], 0).astype(jnp.bfloat16)
+        for b in range(cells_z // LANES):
+            packed[s, b] = stacked[:, b * LANES : (b + 1) * LANES]
+        if s < stages:
+            for c in range(comps):
+                y_send[s, 0, c : c + 1, :] = values[c][0:1, :]
+                y_send[s, 1, c : c + 1, :] = values[c][cells_y - 1 : cells_y, :]
+            for c in range(comps, 8):
+                y_send[s, 0, c : c + 1, :] = jnp.zeros((1, cells_z), jnp.float32)
+                y_send[s, 1, c : c + 1, :] = jnp.zeros((1, cells_z), jnp.float32)
+
+    def unpack(ref):
+        blocks = [ref[b].astype(jnp.float32) for b in range(cells_z // LANES)]
+        return [
+            jnp.concatenate([x[c * cells_y : (c + 1) * cells_y, :] for x in blocks], 1)
+            for c in range(comps)
+        ]
 
     fields_load.wait()
-    current = [state[0, c] for c in range(comps)]
+    current = [start[c] for c in range(comps)]
     put_state(0, current)
     pl.semaphore_wait(barrier, wide + narrow - 2)
 
@@ -226,17 +236,13 @@
             copy.start()
         return started
 
-    def send_snapshot(s, values):
-        stacked = jnp.concatenate(values + [jnp.zeros((snap_out.shape[2] - comps * cells_y, cells_z), jnp.float32)], 0)
-        stacked = stacked.astype(jnp.bfloat16)
-        for b in range(cells_z // LANES):
-            snap_out[s, b] = stacked[:, b * LANES : (b + 1) * LANES]
-        snap_in[s, jn] = snap_out[s, (jn * z_own) // LANES]
+    def send_snapshot(s):
+        snap_in[s, jn] = packed[s + 1, (jn * z_own) // LANES]
         started = []
         for d in range(1, narrow):
             peer = n_peer(d)
             started.append(
-                remote(snap_out.at[s, (peer * z_own) // LANES], snap_in.at[s, jn],
+                remote(packed.at[s + 1, (peer * z_own) // LANES], snap_in.at[s, jn],
                        snap_send.at[s, d], snap_recv.at[s, jn], (iw, peer))
             )
         for copy in started:
@@ -254,19 +260,20 @@
     pick_row = lax.broadcasted_iota(jnp.int32, (16 * groups, LANES), 0)
     pick_z = lax.broadcasted_iota(jnp.int32, (16 * groups, LANES), 1) - offset
     inside = (pick_z >= 0) & (pick_z // z_group == pick_row // 16)
-    acc = [jnp.zeros((16 * groups, LANES), jnp.float32) for _ in range(comps)]
 
     def order_snapshot(s):
         for d in range(1, narrow):
             peer = n_peer(d)
-            remote(snap_out.at[s, 0], snap_in.at[s, peer], snap_send.at[s, d], snap_recv.at[s, peer], (iw, peer)).wait_recv()
+            remote(packed.at[s + 1, 0], snap_in.at[s, peer], snap_send.at[s, d], snap_recv.at[s, peer], (iw, peer)).wait_recv()
         arrived = [snap_in[s, n].astype(jnp.float32) for n in range(narrow)]
         pick = (inside & (lax.rem(pick_row, 16) == 16 - stages + s)).astype(jnp.bfloat16)
         for c in range(comps):
             cells = jnp.concatenate([a[c * cells_y : (c + 1) * cells_y, :] for a in arrived], 0)
             wide_cells = jnp.dot(spread, cells.astype(jnp.bfloat16), preferred_element_type=jnp.float32)
             chosen = jnp.where(fits, wide_cells, 0.0).astype(jnp.bfloat16)
-            acc[c] = acc[c] + lax.dot_general(pick, chosen, NT, preferred_element_type=jnp.float32)
+            ordered = lax.dot_general(pick, chosen, NT, preferred_element_type=jnp.float32)
+            flat = jnp.concatenate([ordered[16 * g : 16 * g + 16, :] for g in range(groups)], 1)
+            tail[c] = (tail[c].astype(jnp.float32) + flat).astype(jnp.bfloat16)
 
     tiles, pivots = [], []
     inverse_cells = 1.0 / (wide * narrow * cells_y * cells_z)
@@ -285,8 +292,8 @@
     for s in range(stages):
         for copy in copies:
             copy.wait_recv()
-        x_low = [x_halo[s, 0, c] for c in range(comps)]
-        x_high = [x_halo[s, 1, c] for c in range(comps)]
+        x_low = unpack(x_halo.at[s, 0])
+        x_high = unpack(x_halo.at[s, 1])
         y_low, y_high = [], []
         for c in range(comps):
             low = jnp.broadcast_to(y_halo[s, 0, c : c + 1, :], (cells_y, cells_z))
@@ -299,28 +306,32 @@
             moved = [0.5 * a + 0.5 * b for a, b in zip(base, moved)]
             base = moved
         current = moved
+        put_state(s + 1, current)
         if s + 1 < stages:
-            put_state(s + 1, current)
             copies = halo_copies(s + 1)
             for copy in copies:
                 copy.start()
             pending += copies
-        pending += send_snapshot(s, current)
-        pending += reduce_step(s + 1)
+        pending += send_snapshot(s)
+        if s == 0:
+            pending += reduce_step(1)
+            pending += reduce_step(2)
+        if s == 1:
+            reduce_step(3)
+            begin()
+            run(0, 3)
+        if s == 2:
+            run(3, 6)
         if s > 0:
             order_snapshot(s - 1)
-        if s == stages - 2:
-            begin()
-            run(0, 4)
     for c in range(comps):
         flow[c] = current[c]
 
-    run(4, 8)
+    run(6, 9)
     order_snapshot(stages - 1)
     total = jnp.zeros((16, columns), jnp.float32)
     for c in range(comps):
-        flat = jnp.concatenate([acc[c][16 * g : 16 * g + 16, :] for g in range(groups)], 1)
-        rows = (tail[c].astype(jnp.float32) + flat).astype(jnp.bfloat16)
+        rows = tail[c]
         x = jnp.concatenate([modes[c, 0:keep, :], rows], 0)
         total = total + lax.dot_general(rows, x, NT, preferred_element_type=jnp.float32)
     mine8 = total[8:16, :]
@@ -333,7 +344,7 @@
     for copy in started:
         copy.start()
     pending += started
-    run(8, 12)
+    run(9, 12)
     for d in range(1, narrow):
         peer = n_peer(d)
         remote(rows8, rows_n.at[peer], last_send.at[0, d], last_recv.at[0, peer], (iw, peer)).wait_recv()
@@ -405,16 +416,16 @@
             jax.ShapeDtypeStruct((comps, cells_y, cells_z), f32),
             jax.ShapeDtypeStruct((columns, columns), f32),
         ),
-        in_specs=[pl.BlockSpec(memory_space=pl.ANY)] * 2,
+        in_specs=[pl.BlockSpec(memory_space=pltpu.HBM)] * 2,
         out_specs=(vmem, vmem),
         scratch_shapes=[
-            pltpu.VMEM(modes.shape, bf16), dma((comps,)), dma((1,)),
-            pltpu.VMEM((stages, comps, cells_y, cells_z), f32),
-            pltpu.VMEM((stages, 2, comps, cells_y, cells_z), f32),
+            pltpu.VMEM(modes.shape, bf16), dma((comps,)),
+            pltpu.VMEM((comps, cells_y, cells_z), f32), dma((1,)),
+            pltpu.VMEM((stages + 1, cells_z // LANES, snap_rows, LANES), bf16),
+            pltpu.VMEM((stages, 2, cells_z // LANES, snap_rows, LANES), bf16),
             pltpu.VMEM((stages, 2, 8, cells_z), f32),
             pltpu.VMEM((stages, 2, 8, cells_z), f32),
             dma((stages, 4)), dma((stages, 4)),
-            pltpu.VMEM((stages, cells_z // LANES, snap_rows, LANES), bf16),
             pltpu.VMEM((stages, narrow, snap_rows, LANES), bf16),
             dma((stages, narrow)), dma((stages, narrow)),
             pltpu.VMEM((columns, columns), f32),
@@ -432,7 +443,7 @@
             dma((2, max(wide, narrow))), dma((2, max(wide, narrow))),
         ],
         compiler_params=pltpu.CompilerParams(
-            collective_id=0, has_side_effects=True, vmem_limit_bytes=60 * 1024 * 1024
+            collective_id=0, has_side_effects=True, vmem_limit_bytes=52 * 1024 * 1024
         ),
     )(fields.reshape(comps, cells_y, cells_z), modes)
     return flow.reshape(fields.shape), factor

time: 38.4 us -> 41.4 us (1.078)
  Pallas kernels: 34.7 us -> 38.6 us
  local copies, waits for them, and re-layouts: 2.87 us -> 2.02 us
    pallas_call x1, Pallas kernels: 34.7 us -> 38.6 us  [local(): pl.pallas_call(functools.partial(kernel, wide, narrow), out_shape=(jax.Sh...]
    unnamed x2 -> x4, local copies, waits for them, and re-layouts: 2.87 us -> 2.02 us
where the time goes in v3:
time: 41.4 us; the launch traced here: 41.2 us
  Pallas kernels  38.6 us (93%)
  local copies, waits for them, and re-layouts  2.02 us (5%)
  between operations  0.65 us (2%)
    pallas_call x1, Pallas kernels, local(): pl.pallas_call(functools.partial(kernel, wide, narrow), out_shape=(jax.Sh...  38.6 us
    unnamed x4, local copies, waits for them, and re-layouts  2.02 us

profile of v3, /device:TPU:0, one launch (start us, length us, event | category | flops | bytes accessed | tf_op | source)
XLA Modules:
  0.0 41.2 jit_solution(13498788922361642052)
XLA Ops:
  0.6 0.0 copy-start
  0.6 0.8 %copy-done = f32[5,1,8,256]{3,2,1,0:T(8,128)S(1)} copy-done((f32[5,1,8,256]{3,2,1,0:T(8,128)S(1)}, f32[5,1,8,256]{3,2,1,0:T(8,128)}, u32[]{:S(2)}) %copy-start) | copy-done | bytes 40984
  1.4 38.6 %shard_map.41 = (f32[5,8,256]{2,1,0:T(8,128)S(1)}, f32[128,128]{1,0:T(8,128)S(1)}) custom-call(f32[5,8,256]{2,1,0:T(8,128)S(1)} %bitcast.10, bf16[5,124,2048]{2,1,0:T(8,128)(2,1)} %bitcast.11), custom_call_target="tpu_custom_call" | custom-call | tf_op jit(solution)/shard_map/pallas_call | solution.py:413
  40.0 0.6 %copy.8 = f32[5,1,8,256]{3,2,1,0:T(8,128)} copy(f32[5,1,8,256]{3,2,1,0:T(8,128)S(1)} %bitcast.9) | data formatting | bytes 81920
  40.6 0.6 %copy.9 = f32[128,128]{1,0:T(8,128)} copy(f32[128,128]{1,0:T(8,128)S(1)} %get-tuple-element.11) | data formatting | bytes 131072
Async XLA Ops:
  0.6 0.8 %copy-start = (f32[5,1,8,256]{3,2,1,0:T(8,128)S(1)}, f32[5,1,8,256]{3,2,1,0:T(8,128)}, u32[]{:S(2)}) copy-start(f32[5,1,8,256]{3,2,1,0:T(8,128)} %param.2) | copy-start | bytes 122884

commit v4 on v3

--- a/solution.py
+++ b/solution.py
@@ -177,21 +177,24 @@
     fields_load.wait()
     current = [start[c] for c in range(comps)]
     put_state(0, current)
-    pl.semaphore_wait(barrier, wide + narrow - 2)
-
-    copies = halo_copies(0)
-    for copy in copies:
-        copy.start()
-    pending = list(copies)
-
-    total = jnp.zeros((columns, columns), jnp.float32)
-    for c in range(comps):
+    def gram_part(c):
         loads[c].wait()
         last = modes[c, keep:prior, :].astype(jnp.float32)
         last = jnp.concatenate([last, jnp.zeros((columns - prior, mode_lanes), jnp.float32)], 0)
         tail[c] = last.astype(jnp.bfloat16)
         x = jnp.concatenate([modes[c, 0:keep, :], tail[c]], 0)
-        total = total + lax.dot_general(x, x, NT, preferred_element_type=jnp.float32)
+        return lax.dot_general(x, x, NT, preferred_element_type=jnp.float32)
+
+    total = gram_part(0)
+    pl.semaphore_wait(barrier, wide + narrow - 2)
+
+    copies = halo_copies(0)
+    for copy in copies:
+        copy.start()
+    pending = list(copies)
+
+    for c in range(1, comps):
+        total = total + gram_part(c)
     gram[...] = total
     mine = pl.ds(pl.multiple_of(iw * piece_rows, piece_rows), piece_rows)
     scatter[iw] = gram[mine, :]
@@ -251,11 +254,11 @@
 
     offset = lax.rem(jn * z_own, LANES)
     spread = (
-        lax.rem(lax.broadcasted_iota(jnp.int32, (LANES, y_all), 0), y_all)
-        == lax.broadcasted_iota(jnp.int32, (LANES, y_all), 1)
+        lax.rem(lax.broadcasted_iota(jnp.int32, (y_all, LANES), 1), y_all)
+        == lax.broadcasted_iota(jnp.int32, (y_all, LANES), 0)
     ).astype(jnp.bfloat16)
-    z_id = lax.broadcasted_iota(jnp.int32, (LANES, LANES), 1) - offset
-    k_id = lax.broadcasted_iota(jnp.int32, (LANES, LANES), 0) // y_all
+    z_id = lax.broadcasted_iota(jnp.int32, (LANES, LANES), 0) - offset
+    k_id = lax.broadcasted_iota(jnp.int32, (LANES, LANES), 1) // y_all
     fits = lax.rem(z_id + LANES, z_group) == k_id
     pick_row = lax.broadcasted_iota(jnp.int32, (16 * groups, LANES), 0)
     pick_z = lax.broadcasted_iota(jnp.int32, (16 * groups, LANES), 1) - offset
@@ -269,9 +272,11 @@
         pick = (inside & (lax.rem(pick_row, 16) == 16 - stages + s)).astype(jnp.bfloat16)
         for c in range(comps):
             cells = jnp.concatenate([a[c * cells_y : (c + 1) * cells_y, :] for a in arrived], 0)
-            wide_cells = jnp.dot(spread, cells.astype(jnp.bfloat16), preferred_element_type=jnp.float32)
+            wide_cells = lax.dot_general(
+                cells.astype(jnp.bfloat16), spread, (((0,), (0,)), ((), ())), preferred_element_type=jnp.float32
+            )
             chosen = jnp.where(fits, wide_cells, 0.0).astype(jnp.bfloat16)
-            ordered = lax.dot_general(pick, chosen, NT, preferred_element_type=jnp.float32)
+            ordered = jnp.dot(pick, chosen, preferred_element_type=jnp.float32)
             flat = jnp.concatenate([ordered[16 * g : 16 * g + 16, :] for g in range(groups)], 1)
             tail[c] = (tail[c].astype(jnp.float32) + flat).astype(jnp.bfloat16)
 
@@ -313,28 +318,23 @@
                 copy.start()
             pending += copies
         pending += send_snapshot(s)
-        if s == 0:
-            pending += reduce_step(1)
-            pending += reduce_step(2)
-        if s == 1:
-            reduce_step(3)
-            begin()
-            run(0, 3)
-        if s == 2:
-            run(3, 6)
+        pending += reduce_step(s + 1)
         if s > 0:
             order_snapshot(s - 1)
+        if s == stages - 2:
+            begin()
+            run(0, 4)
     for c in range(comps):
         flow[c] = current[c]
 
-    run(6, 9)
+    run(4, 8)
     order_snapshot(stages - 1)
-    total = jnp.zeros((16, columns), jnp.float32)
+    total = jnp.zeros((columns, 16), jnp.float32)
     for c in range(comps):
         rows = tail[c]
         x = jnp.concatenate([modes[c, 0:keep, :], rows], 0)
-        total = total + lax.dot_general(rows, x, NT, preferred_element_type=jnp.float32)
-    mine8 = total[8:16, :]
+        total = total + lax.dot_general(x, rows, NT, preferred_element_type=jnp.float32)
+    mine8 = jnp.transpose(total)[8:16, :]
     rows8[...] = mine8
     rows_n[jn] = mine8
     started = [
@@ -344,7 +344,7 @@
     for copy in started:
         copy.start()
     pending += started
-    run(9, 12)
+    run(8, 12)
     for d in range(1, narrow):
         peer = n_peer(d)
         remote(rows8, rows_n.at[peer], last_send.at[0, d], last_recv.at[0, peer], (iw, peer)).wait_recv()

time: 41.4 us -> 37.6 us (0.908)
  Pallas kernels: 38.6 us -> 34.7 us
    pallas_call x1, Pallas kernels: 38.6 us -> 34.7 us  [local(): pl.pallas_call(functools.partial(kernel, wide, narrow), out_shape=(jax.Sh...]
where the time goes in v4:
time: 37.6 us; the launch traced here: 37.4 us
  Pallas kernels  34.7 us (92%)
  local copies, waits for them, and re-layouts  2.02 us (5%)
  between operations  0.65 us (2%)
    pallas_call x1, Pallas kernels, local(): pl.pallas_call(functools.partial(kernel, wide, narrow), out_shape=(jax.Sh...  34.7 us
    unnamed x4, local copies, waits for them, and re-layouts  2.02 us

profile of v4, /device:TPU:0, one launch (start us, length us, event | category | flops | bytes accessed | tf_op | source)
XLA Modules:
  0.0 37.4 jit_solution(1943410908202400881)
XLA Ops:
  0.6 0.0 copy-start
  0.6 0.8 %copy-done = f32[5,1,8,256]{3,2,1,0:T(8,128)S(1)} copy-done((f32[5,1,8,256]{3,2,1,0:T(8,128)S(1)}, f32[5,1,8,256]{3,2,1,0:T(8,128)}, u32[]{:S(2)}) %copy-start) | copy-done | bytes 40984
  1.4 34.7 %shard_map.41 = (f32[5,8,256]{2,1,0:T(8,128)S(1)}, f32[128,128]{1,0:T(8,128)S(1)}) custom-call(f32[5,8,256]{2,1,0:T(8,128)S(1)} %bitcast.10, bf16[5,124,2048]{2,1,0:T(8,128)(2,1)} %bitcast.11), custom_call_target="tpu_custom_call" | custom-call | tf_op jit(solution)/shard_map/pallas_call | solution.py:413
  36.2 0.6 %copy.8 = f32[5,1,8,256]{3,2,1,0:T(8,128)} copy(f32[5,1,8,256]{3,2,1,0:T(8,128)S(1)} %bitcast.9) | data formatting | bytes 81920
  36.8 0.6 %copy.9 = f32[128,128]{1,0:T(8,128)} copy(f32[128,128]{1,0:T(8,128)S(1)} %get-tuple-element.11) | data formatting | bytes 131072
Async XLA Ops:
  0.6 0.8 %copy-start = (f32[5,1,8,256]{3,2,1,0:T(8,128)S(1)}, f32[5,1,8,256]{3,2,1,0:T(8,128)}, u32[]{:S(2)}) copy-start(f32[5,1,8,256]{3,2,1,0:T(8,128)} %param.2) | copy-start | bytes 122884

commit v5 on v4

--- a/solution.py
+++ b/solution.py
@@ -28,19 +28,18 @@
     return out
 
 
-def tendency(here, x_low, x_high, y_low, y_high):
+def along(low, high, d):
+    return [
+        -0.5 * (fh - fl) + VISCOSITY * (l + h)
+        for fh, fl, l, h in zip(flux_of(high, d), flux_of(low, d), low, high)
+    ]
+
+
+def inner_part(here):
     cells_z = here[0].shape[1]
     z_low = [pltpu.roll(c, 1, 1) for c in here]
     z_high = [pltpu.roll(c, cells_z - 1, 1) for c in here]
-    total = None
-    for d, (low, high) in enumerate(((x_low, x_high), (y_low, y_high), (z_low, z_high))):
-        flux_low, flux_high = flux_of(low, d), flux_of(high, d)
-        part = [
-            -0.5 * (fh - fl) + VISCOSITY * (l + h)
-            for fh, fl, l, h in zip(flux_high, flux_low, low, high)
-        ]
-        total = part if total is None else [a + b for a, b in zip(total, part)]
-    return [t - (6.0 * VISCOSITY) * c for t, c in zip(total, here)]
+    return [a - (6.0 * VISCOSITY) * c for a, c in zip(along(z_low, z_high, 2), here)]
 
 
 def lane_ids():
@@ -67,35 +66,39 @@
 
 def eliminate_panel(tiles, p, first, last):
     lane, row = lane_ids(), row_ids()
-    pivots = jnp.zeros((8, LANES), jnp.float32)
     steps = range(first, last)
     panel = tiles[p]
-    columns = {k: column_of(panel, 8 * p + k) for k in steps}
-    heads, inverses, crossings = {}, {}, {}
+    inside = (lane >= 8 * p + first) & (lane < 8 * p + last)
+    spread = {k: column_of(panel, 8 * p + k) for k in steps}
+    entry = {(m, k): row_of(spread[k], m) for k in steps for m in range(k, last)}
+    inverses, ratio = {}, {}
     for k in steps:
-        j = 8 * p + k
-        pivot = row_of(columns[k], k)
-        inverses[k] = inverted(pivot)
-        pivots = jnp.where(row == k, pivot, pivots)
-        factor = jnp.where(row > k, columns[k], 0.0) * inverses[k]
-        for m in steps:
-            if m > k:
-                crossings[k, m] = row_of(columns[m], k)
-                columns[m] = columns[m] - factor * crossings[k, m]
-        heads[k] = jnp.where(lane == j, 1.0, row_of(panel, k))
-        panel = jnp.where((lane == j) & (row > k), 0.0, panel) - factor * heads[k]
+        inverses[k] = inverted(entry[k, k])
+        for m in range(k + 1, last):
+            ratio[m, k] = entry[m, k] * inverses[k]
+            for n in range(m, last):
+                entry[n, m] = entry[n, m] - entry[n, k] * ratio[m, k]
+    raw = {k: row_of(panel, k) for k in steps}
+    heads = {k: jnp.where(inside, jnp.where(lane == 8 * p + k, 1.0, 0.0), raw[k]) for k in steps}
+    for k in steps:
+        for m in range(first, k):
+            raw[k] = raw[k] - ratio[k, m] * raw[m]
+            heads[k] = heads[k] - ratio[k, m] * heads[m]
+    pivots = jnp.zeros((8, LANES), jnp.float32)
+    panel = jnp.zeros((8, LANES), jnp.float32)
+    for k in steps:
+        pivots = jnp.where(row == k, entry[k, k], pivots)
+        panel = jnp.where(row == k, jnp.where(inside & (lane < 8 * p + k), heads[k], raw[k]), panel)
     tiles[p] = panel
-    cleared = (lane >= 8 * p + first) & (lane < 8 * p + last)
     for t in range(p + 1, len(tiles)):
-        columns = {k: column_of(tiles[t], 8 * p + k) for k in steps}
-        rest = jnp.where(cleared, 0.0, tiles[t])
+        rest = jnp.where(inside, 0.0, tiles[t])
+        factors = {}
         for k in steps:
-            factor = columns[k] * inverses[k]
-            for m in steps:
-                if m > k:
-                    columns[m] = columns[m] - factor * crossings[k, m]
-            outside = jnp.where((lane > 8 * p + k) & cleared, 0.0, heads[k])
-            rest = rest - factor * outside
+            left = column_of(tiles[t], 8 * p + k)
+            for m in range(first, k):
+                left = left - factors[m] * entry[k, m]
+            factors[k] = left * inverses[k]
+            rest = rest - factors[k] * heads[k]
         tiles[t] = rest
     return pivots
 
@@ -295,6 +298,9 @@
     row = lax.broadcasted_iota(jnp.int32, (cells_y, cells_z), 0)
     base = current
     for s in range(stages):
+        inner = inner_part(current)
+        below = [pltpu.roll(c, 1, 0) for c in current]
+        above = [pltpu.roll(c, cells_y - 1, 0) for c in current]
         for copy in copies:
             copy.wait_recv()
         x_low = unpack(x_halo.at[s, 0])
@@ -303,9 +309,11 @@
         for c in range(comps):
             low = jnp.broadcast_to(y_halo[s, 0, c : c + 1, :], (cells_y, cells_z))
             high = jnp.broadcast_to(y_halo[s, 1, c : c + 1, :], (cells_y, cells_z))
-            y_low.append(jnp.where(row == 0, low, pltpu.roll(current[c], 1, 0)))
-            y_high.append(jnp.where(row == cells_y - 1, high, pltpu.roll(current[c], cells_y - 1, 0)))
-        change = tendency(current, x_low, x_high, y_low, y_high)
+            y_low.append(jnp.where(row == 0, low, below[c]))
+            y_high.append(jnp.where(row == cells_y - 1, high, above[c]))
+        change = [
+            a + b + c for a, b, c in zip(inner, along(x_low, x_high, 0), along(y_low, y_high, 1))
+        ]
         moved = [a + TIME_STEP * b for a, b in zip(current, change)]
         if s % 2 == 1:
             moved = [0.5 * a + 0.5 * b for a, b in zip(base, moved)]

time: 37.6 us -> 37.6 us (level)
  no operation moved by 1% of the time
where the time goes in v5:
time: 37.6 us; the launch traced here: 37.4 us
  Pallas kernels  34.8 us (93%)
  local copies, waits for them, and re-layouts  2.02 us (5%)
  between operations  0.65 us (2%)
    pallas_call x1, Pallas kernels, local(): pl.pallas_call(functools.partial(kernel, wide, narrow), out_shape=(jax.Sh...  34.8 us
    unnamed x4, local copies, waits for them, and re-layouts  2.02 us

profile of v5, /device:TPU:0, one launch (start us, length us, event | category | flops | bytes accessed | tf_op | source)
XLA Modules:
  0.0 37.4 jit_solution(11407435761475894103)
XLA Ops:
  0.6 0.0 copy-start
  0.6 0.8 %copy-done = f32[5,1,8,256]{3,2,1,0:T(8,128)S(1)} copy-done((f32[5,1,8,256]{3,2,1,0:T(8,128)S(1)}, f32[5,1,8,256]{3,2,1,0:T(8,128)}, u32[]{:S(2)}) %copy-start) | copy-done | bytes 40984
  1.4 34.8 %shard_map.41 = (f32[5,8,256]{2,1,0:T(8,128)S(1)}, f32[128,128]{1,0:T(8,128)S(1)}) custom-call(f32[5,8,256]{2,1,0:T(8,128)S(1)} %bitcast.10, bf16[5,124,2048]{2,1,0:T(8,128)(2,1)} %bitcast.11), custom_call_target="tpu_custom_call" | custom-call | tf_op jit(solution)/shard_map/pallas_call | solution.py:421
  36.2 0.6 %copy.8 = f32[5,1,8,256]{3,2,1,0:T(8,128)} copy(f32[5,1,8,256]{3,2,1,0:T(8,128)S(1)} %bitcast.9) | data formatting | bytes 81920
  36.8 0.6 %copy.9 = f32[128,128]{1,0:T(8,128)} copy(f32[128,128]{1,0:T(8,128)S(1)} %get-tuple-element.11) | data formatting | bytes 131072
Async XLA Ops:
  0.6 0.8 %copy-start = (f32[5,1,8,256]{3,2,1,0:T(8,128)S(1)}, f32[5,1,8,256]{3,2,1,0:T(8,128)}, u32[]{:S(2)}) copy-start(f32[5,1,8,256]{3,2,1,0:T(8,128)} %param.2) | copy-start | bytes 122884

commit v6 on v5

--- a/solution.py
+++ b/solution.py
@@ -105,7 +105,7 @@
 
 def kernel(
     wide, narrow, fields, modes_hbm, flow, factor_out,
-    modes, modes_sem, start, start_sem, packed, x_halo, y_send, y_halo, halo_send, halo_recv,
+    modes, modes_sem, start, start_sem, packed, x_halo, y_send, y_halo, d_halo, halo_send, halo_recv,
     snap_in, snap_send, snap_recv,
     gram, scatter, part, share, whole, piece, red_send, red_recv,
     tail, rows8, rows_n, sums8, rows_w, last_send, last_recv,
@@ -123,11 +123,14 @@
     keep = columns - 16
     iw, jn = lax.axis_index("wide"), lax.axis_index("narrow")
 
+    w_peers = [lax.rem(iw + d, wide) for d in range(wide)]
+    n_peers = [lax.rem(jn + d, narrow) for d in range(narrow)]
+
     def w_peer(d):
-        return lax.rem(iw + d, wide)
+        return w_peers[d % wide]
 
     def n_peer(d):
-        return lax.rem(jn + d, narrow)
+        return n_peers[d % narrow]
 
     def remote(src, dst, send, recv, device):
         return pltpu.make_async_remote_copy(
@@ -147,14 +150,21 @@
     for d in range(1, narrow):
         pl.semaphore_signal(barrier, inc=1, device_id=(iw, n_peer(d)), device_id_type=pl.DeviceIdType.MESH)
 
-    def halo_copies(s):
-        right, left = (w_peer(1), jn), (w_peer(wide - 1), jn)
-        up, down = (iw, n_peer(1)), (iw, n_peer(narrow - 1))
+    for d in (1, wide - 1):
+        for e in (1, narrow - 1):
+            pl.semaphore_signal(barrier, inc=1, device_id=(w_peer(d), n_peer(e)), device_id_type=pl.DeviceIdType.MESH)
+
+    def halo_copies(q):
+        moves = []
+        for side, d in enumerate((1, -1, 2, -2)):
+            moves.append((packed.at[2 * q], x_halo.at[q, side], (w_peer(d), jn)))
+        for e, y_side in ((1, 0), (-1, 1)):
+            moves.append((y_send.at[q, 1 - y_side], y_halo.at[q, y_side], (iw, n_peer(e))))
+            for d, x_side in ((1, 0), (-1, 1)):
+                moves.append((y_send.at[q, 1 - y_side, 0], d_halo.at[q, x_side, y_side], (w_peer(d), n_peer(e))))
         return [
-            remote(packed.at[s], x_halo.at[s, 0], halo_send.at[s, 0], halo_recv.at[s, 0], right),
-            remote(packed.at[s], x_halo.at[s, 1], halo_send.at[s, 1], halo_recv.at[s, 1], left),
-            remote(y_send.at[s, 1], y_halo.at[s, 0], halo_send.at[s, 2], halo_recv.at[s, 2], up),
-            remote(y_send.at[s, 0], y_halo.at[s, 1], halo_send.at[s, 3], halo_recv.at[s, 3], down),
+            remote(src, dst, halo_send.at[q, i], halo_recv.at[q, i], device)
+            for i, (src, dst, device) in enumerate(moves)
         ]
 
     def put_state(s, values):
@@ -162,13 +172,15 @@
         stacked = jnp.concatenate(values + [spare], 0).astype(jnp.bfloat16)
         for b in range(cells_z // LANES):
             packed[s, b] = stacked[:, b * LANES : (b + 1) * LANES]
-        if s < stages:
-            for c in range(comps):
-                y_send[s, 0, c : c + 1, :] = values[c][0:1, :]
-                y_send[s, 1, c : c + 1, :] = values[c][cells_y - 1 : cells_y, :]
-            for c in range(comps, 8):
-                y_send[s, 0, c : c + 1, :] = jnp.zeros((1, cells_z), jnp.float32)
-                y_send[s, 1, c : c + 1, :] = jnp.zeros((1, cells_z), jnp.float32)
+        if s % 2 == 0 and s < stages:
+            for depth in range(2):
+                for c in range(comps):
+                    y_send[s // 2, 0, depth, c : c + 1, :] = values[c][depth : depth + 1, :]
+                    top = cells_y - 1 - depth
+                    y_send[s // 2, 1, depth, c : c + 1, :] = values[c][top : top + 1, :]
+                for c in range(comps, 8):
+                    y_send[s // 2, 0, depth, c : c + 1, :] = jnp.zeros((1, cells_z), jnp.float32)
+                    y_send[s // 2, 1, depth, c : c + 1, :] = jnp.zeros((1, cells_z), jnp.float32)
 
     def unpack(ref):
         blocks = [ref[b].astype(jnp.float32) for b in range(cells_z // LANES)]
@@ -189,7 +201,7 @@
         return lax.dot_general(x, x, NT, preferred_element_type=jnp.float32)
 
     total = gram_part(0)
-    pl.semaphore_wait(barrier, wide + narrow - 2)
+    pl.semaphore_wait(barrier, wide + narrow + 2)
 
     copies = halo_copies(0)
     for copy in copies:
@@ -296,46 +308,76 @@
             pivots.append(eliminate_panel(tiles, p, 0, min(8, prior - 8 * p)))
 
     row = lax.broadcasted_iota(jnp.int32, (cells_y, cells_z), 0)
-    base = current
-    for s in range(stages):
+
+    def line(values, k):
+        return [jnp.broadcast_to(v[k : k + 1, :], (cells_y, cells_z)) for v in values]
+
+    def lines(ref):
+        return [jnp.broadcast_to(ref[c : c + 1, :], (cells_y, cells_z)) for c in range(comps)]
+
+    def either(low, high):
+        return [jnp.where(row == 0, a, b) for a, b in zip(low, high)]
+
+    def shifted(here, low, high):
+        below = [jnp.where(row == 0, a, pltpu.roll(c, 1, 0)) for a, c in zip(low, here)]
+        above = [
+            jnp.where(row == cells_y - 1, a, pltpu.roll(c, cells_y - 1, 0)) for a, c in zip(high, here)
+        ]
+        return below, above
+
+    def change_of(inner, x_low, x_high, y_low, y_high):
+        return [a + b + c for a, b, c in zip(inner, along(x_low, x_high, 0), along(y_low, y_high, 1))]
+
+    def moved(here, inner, x_low, x_high, y_low, y_high):
+        change = change_of(inner, x_low, x_high, y_low, y_high)
+        return [a + TIME_STEP * b for a, b in zip(here, change)]
+
+    for q in range(STEPS):
         inner = inner_part(current)
-        below = [pltpu.roll(c, 1, 0) for c in current]
-        above = [pltpu.roll(c, cells_y - 1, 0) for c in current]
         for copy in copies:
             copy.wait_recv()
-        x_low = unpack(x_halo.at[s, 0])
-        x_high = unpack(x_halo.at[s, 1])
-        y_low, y_high = [], []
-        for c in range(comps):
-            low = jnp.broadcast_to(y_halo[s, 0, c : c + 1, :], (cells_y, cells_z))
-            high = jnp.broadcast_to(y_halo[s, 1, c : c + 1, :], (cells_y, cells_z))
-            y_low.append(jnp.where(row == 0, low, below[c]))
-            y_high.append(jnp.where(row == cells_y - 1, high, above[c]))
-        change = [
-            a + b + c for a, b, c in zip(inner, along(x_low, x_high, 0), along(y_low, y_high, 1))
-        ]
-        moved = [a + TIME_STEP * b for a, b in zip(current, change)]
-        if s % 2 == 1:
-            moved = [0.5 * a + 0.5 * b for a, b in zip(base, moved)]
-            base = moved
-        current = moved
-        put_state(s + 1, current)
-        if s + 1 < stages:
-            copies = halo_copies(s + 1)
+        planes = [unpack(x_halo.at[q, side]) for side in range(4)]
+        low, high = lines(y_halo.at[q, 0, 0]), lines(y_halo.at[q, 1, 0])
+        corner = [[lines(d_halo.at[q, i, j]) for j in range(2)] for i in range(2)]
+        first_own = moved(current, inner, planes[0], planes[1], *shifted(current, low, high))
+        put_state(2 * q + 1, first_own)
+        pending += send_snapshot(2 * q)
+        first_low = moved(
+            planes[0], inner_part(planes[0]), planes[2], current, *shifted(planes[0], *corner[0])
+        )
+        first_high = moved(
+            planes[1], inner_part(planes[1]), current, planes[3], *shifted(planes[1], *corner[1])
+        )
+        rim = either(low, high)
+        first_rim = moved(
+            rim, inner_part(rim), either(*corner[0]), either(*corner[1]),
+            either(lines(y_halo.at[q, 0, 1]), line(current, cells_y - 1)),
+            either(line(current, 0), lines(y_halo.at[q, 1, 1])),
+        )
+        second = moved(
+            first_own, inner_part(first_own), first_low, first_high,
+            *shifted(first_own, line(first_rim, 0), line(first_rim, 1)),
+        )
+        current = [0.5 * a + 0.5 * b for a, b in zip(current, second)]
+        put_state(2 * q + 2, current)
+        if q + 1 < STEPS:
+            copies = halo_copies(q + 1)
             for copy in copies:
                 copy.start()
             pending += copies
-        pending += send_snapshot(s)
-        pending += reduce_step(s + 1)
-        if s > 0:
-            order_snapshot(s - 1)
-        if s == stages - 2:
-            begin()
-            run(0, 4)
+        pending += send_snapshot(2 * q + 1)
+        if q == 0:
+            pending += reduce_step(1)
+            order_snapshot(0)
+            pending += reduce_step(2)
+    reduce_step(3)
+    begin()
+    run(0, 3)
+    for s in range(1, stages - 1):
+        order_snapshot(s)
     for c in range(comps):
         flow[c] = current[c]
 
-    run(4, 8)
     order_snapshot(stages - 1)
     total = jnp.zeros((columns, 16), jnp.float32)
     for c in range(comps):
@@ -352,7 +394,7 @@
     for copy in started:
         copy.start()
     pending += started
-    run(8, 12)
+    run(3, 9)
     for d in range(1, narrow):
         peer = n_peer(d)
         remote(rows8, rows_n.at[peer], last_send.at[0, d], last_recv.at[0, peer], (iw, peer)).wait_recv()
@@ -368,7 +410,7 @@
     for copy in started:
         copy.start()
     pending += started
-    run(12, columns // 8)
+    run(9, columns // 8)
     lane, row = lane_ids(), row_ids()
     uppers, inverse = [], []
     for t in range(columns // 8):
@@ -430,10 +472,11 @@
             pltpu.VMEM(modes.shape, bf16), dma((comps,)),
             pltpu.VMEM((comps, cells_y, cells_z), f32), dma((1,)),
             pltpu.VMEM((stages + 1, cells_z // LANES, snap_rows, LANES), bf16),
-            pltpu.VMEM((stages, 2, cells_z // LANES, snap_rows, LANES), bf16),
-            pltpu.VMEM((stages, 2, 8, cells_z), f32),
-            pltpu.VMEM((stages, 2, 8, cells_z), f32),
-            dma((stages, 4)), dma((stages, 4)),
+            pltpu.VMEM((STEPS, 4, cells_z // LANES, snap_rows, LANES), bf16),
+            pltpu.VMEM((STEPS, 2, 2, 8, cells_z), f32),
+            pltpu.VMEM((STEPS, 2, 2, 8, cells_z), f32),
+            pltpu.VMEM((STEPS, 2, 2, 8, cells_z), f32),
+            dma((STEPS, 10)), dma((STEPS, 10)),
             pltpu.VMEM((stages, narrow, snap_rows, LANES), bf16),
             dma((stages, narrow)), dma((stages, narrow)),
             pltpu.VMEM((columns, columns), f32),

time: 37.6 us -> 38.1 us (1.013)
  Pallas kernels: 34.8 us -> 35.2 us
    pallas_call x1, Pallas kernels: 34.8 us -> 35.2 us  [local(): pl.pallas_call(functools.partial(kernel, wide, narrow), out_shape=(jax.Sh...]
where the time goes in v6:
time: 38.1 us; the launch traced here: 37.9 us
  Pallas kernels  35.2 us (92%)
  local copies, waits for them, and re-layouts  2.02 us (5%)
  between operations  0.65 us (2%)
    pallas_call x1, Pallas kernels, local(): pl.pallas_call(functools.partial(kernel, wide, narrow), out_shape=(jax.Sh...  35.2 us
    unnamed x4, local copies, waits for them, and re-layouts  2.02 us

profile of v6, /device:TPU:0, one launch (start us, length us, event | category | flops | bytes accessed | tf_op | source)
XLA Modules:
  0.0 37.9 jit_solution(4451073420682820836)
XLA Ops:
  0.6 0.0 copy-start
  0.6 0.8 %copy-done = f32[5,1,8,256]{3,2,1,0:T(8,128)S(1)} copy-done((f32[5,1,8,256]{3,2,1,0:T(8,128)S(1)}, f32[5,1,8,256]{3,2,1,0:T(8,128)}, u32[]{:S(2)}) %copy-start) | copy-done | bytes 40984
  1.4 35.2 %shard_map.41 = (f32[5,8,256]{2,1,0:T(8,128)S(1)}, f32[128,128]{1,0:T(8,128)S(1)}) custom-call(f32[5,8,256]{2,1,0:T(8,128)S(1)} %bitcast.10, bf16[5,124,2048]{2,1,0:T(8,128)(2,1)} %bitcast.11), custom_call_target="tpu_custom_call" | custom-call | tf_op jit(solution)/shard_map/pallas_call | solution.py:463
  36.6 0.6 %copy.8 = f32[5,1,8,256]{3,2,1,0:T(8,128)} copy(f32[5,1,8,256]{3,2,1,0:T(8,128)S(1)} %bitcast.9) | data formatting | bytes 81920
  37.3 0.6 %copy.9 = f32[128,128]{1,0:T(8,128)} copy(f32[128,128]{1,0:T(8,128)S(1)} %get-tuple-element.11) | data formatting | bytes 131072
Async XLA Ops:
  0.6 0.8 %copy-start = (f32[5,1,8,256]{3,2,1,0:T(8,128)S(1)}, f32[5,1,8,256]{3,2,1,0:T(8,128)}, u32[]{:S(2)}) copy-start(f32[5,1,8,256]{3,2,1,0:T(8,128)} %param.2) | copy-start | bytes 122884

commit v7 on v6

--- a/solution.py
+++ b/solution.py
@@ -254,14 +254,16 @@
             copy.start()
         return started
 
-    def send_snapshot(s):
-        snap_in[s, jn] = packed[s + 1, (jn * z_own) // LANES]
+    def send_snapshots(q):
+        own, made = pl.ds(2 * q, 2), pl.ds(2 * q + 1, 2)
+        for i in range(2):
+            snap_in[2 * q + i, jn] = packed[2 * q + 1 + i, (jn * z_own) // LANES]
         started = []
         for d in range(1, narrow):
             peer = n_peer(d)
             started.append(
-                remote(packed.at[s + 1, (peer * z_own) // LANES], snap_in.at[s, jn],
-                       snap_send.at[s, d], snap_recv.at[s, jn], (iw, peer))
+                remote(packed.at[made, (peer * z_own) // LANES], snap_in.at[own, jn],
+                       snap_send.at[q, d], snap_recv.at[q, jn], (iw, peer))
             )
         for copy in started:
             copy.start()
@@ -279,21 +281,26 @@
     pick_z = lax.broadcasted_iota(jnp.int32, (16 * groups, LANES), 1) - offset
     inside = (pick_z >= 0) & (pick_z // z_group == pick_row // 16)
 
-    def order_snapshot(s):
+    def order_snapshots(q):
+        own, made = pl.ds(2 * q, 2), pl.ds(2 * q + 1, 2)
         for d in range(1, narrow):
             peer = n_peer(d)
-            remote(packed.at[s + 1, 0], snap_in.at[s, peer], snap_send.at[s, d], snap_recv.at[s, peer], (iw, peer)).wait_recv()
-        arrived = [snap_in[s, n].astype(jnp.float32) for n in range(narrow)]
-        pick = (inside & (lax.rem(pick_row, 16) == 16 - stages + s)).astype(jnp.bfloat16)
+            remote(packed.at[made, 0], snap_in.at[own, peer], snap_send.at[q, d], snap_recv.at[q, peer], (iw, peer)).wait_recv()
+        arrived = [[snap_in[2 * q + i, n].astype(jnp.float32) for n in range(narrow)] for i in range(2)]
+        pick = jnp.concatenate(
+            [inside & (lax.rem(pick_row, 16) == 16 - stages + 2 * q + i) for i in range(2)], 1
+        ).astype(jnp.bfloat16)
         for c in range(comps):
-            cells = jnp.concatenate([a[c * cells_y : (c + 1) * cells_y, :] for a in arrived], 0)
-            wide_cells = lax.dot_general(
-                cells.astype(jnp.bfloat16), spread, (((0,), (0,)), ((), ())), preferred_element_type=jnp.float32
-            )
-            chosen = jnp.where(fits, wide_cells, 0.0).astype(jnp.bfloat16)
-            ordered = jnp.dot(pick, chosen, preferred_element_type=jnp.float32)
+            chosen = []
+            for i in range(2):
+                cells = jnp.concatenate([a[c * cells_y : (c + 1) * cells_y, :] for a in arrived[i]], 0)
+                wide_cells = lax.dot_general(
+                    cells.astype(jnp.bfloat16), spread, (((0,), (0,)), ((), ())), preferred_element_type=jnp.float32
+                )
+                chosen.append(jnp.where(fits, wide_cells, 0.0).astype(jnp.bfloat16))
+            ordered = jnp.dot(pick, jnp.concatenate(chosen, 0), preferred_element_type=jnp.float32)
             flat = jnp.concatenate([ordered[16 * g : 16 * g + 16, :] for g in range(groups)], 1)
-            tail[c] = (tail[c].astype(jnp.float32) + flat).astype(jnp.bfloat16)
+            tail[c] = tail[c] + flat.astype(jnp.bfloat16)
 
     tiles, pivots = [], []
     inverse_cells = 1.0 / (wide * narrow * cells_y * cells_z)
@@ -341,7 +348,6 @@
         corner = [[lines(d_halo.at[q, i, j]) for j in range(2)] for i in range(2)]
         first_own = moved(current, inner, planes[0], planes[1], *shifted(current, low, high))
         put_state(2 * q + 1, first_own)
-        pending += send_snapshot(2 * q)
         first_low = moved(
             planes[0], inner_part(planes[0]), planes[2], current, *shifted(planes[0], *corner[0])
         )
@@ -365,20 +371,18 @@
             for copy in copies:
                 copy.start()
             pending += copies
-        pending += send_snapshot(2 * q + 1)
+        pending += send_snapshots(q)
         if q == 0:
             pending += reduce_step(1)
-            order_snapshot(0)
+            order_snapshots(0)
             pending += reduce_step(2)
     reduce_step(3)
     begin()
     run(0, 3)
-    for s in range(1, stages - 1):
-        order_snapshot(s)
     for c in range(comps):
         flow[c] = current[c]
 
-    order_snapshot(stages - 1)
+    order_snapshots(STEPS - 1)
     total = jnp.zeros((columns, 16), jnp.float32)
     for c in range(comps):
         rows = tail[c]
@@ -478,7 +482,7 @@
             pltpu.VMEM((STEPS, 2, 2, 8, cells_z), f32),
             dma((STEPS, 10)), dma((STEPS, 10)),
             pltpu.VMEM((stages, narrow, snap_rows, LANES), bf16),
-            dma((stages, narrow)), dma((stages, narrow)),
+            dma((STEPS, narrow)), dma((STEPS, narrow)),
             pltpu.VMEM((columns, columns), f32),
             pltpu.VMEM((wide, piece, columns), f32),
             pltpu.VMEM((piece, columns), f32),

time: 38.1 us -> 37.5 us (0.984)
  Pallas kernels: 35.2 us -> 34.6 us
    pallas_call x1, Pallas kernels: 35.2 us -> 34.6 us  [local(): pl.pallas_call(functools.partial(kernel, wide, narrow), out_shape=(jax.Sh...]
where the time goes in v7:
time: 37.5 us; the launch traced here: 37.3 us
  Pallas kernels  34.6 us (92%)
  local copies, waits for them, and re-layouts  2.02 us (5%)
  between operations  0.65 us (2%)
    pallas_call x1, Pallas kernels, local(): pl.pallas_call(functools.partial(kernel, wide, narrow), out_shape=(jax.Sh...  34.6 us
    unnamed x4, local copies, waits for them, and re-layouts  2.02 us

profile of v7, /device:TPU:0, one launch (start us, length us, event | category | flops | bytes accessed | tf_op | source)
XLA Modules:
  0.0 37.3 jit_solution(12896551015733614399)
XLA Ops:
  0.6 0.0 copy-start
  0.6 0.8 %copy-done = f32[5,1,8,256]{3,2,1,0:T(8,128)S(1)} copy-done((f32[5,1,8,256]{3,2,1,0:T(8,128)S(1)}, f32[5,1,8,256]{3,2,1,0:T(8,128)}, u32[]{:S(2)}) %copy-start) | copy-done | bytes 40984
  1.4 34.6 %shard_map.41 = (f32[5,8,256]{2,1,0:T(8,128)S(1)}, f32[128,128]{1,0:T(8,128)S(1)}) custom-call(f32[5,8,256]{2,1,0:T(8,128)S(1)} %bitcast.10, bf16[5,124,2048]{2,1,0:T(8,128)(2,1)} %bitcast.11), custom_call_target="tpu_custom_call" | custom-call | tf_op jit(solution)/shard_map/pallas_call | solution.py:467
  36.1 0.6 %copy.8 = f32[5,1,8,256]{3,2,1,0:T(8,128)} copy(f32[5,1,8,256]{3,2,1,0:T(8,128)S(1)} %bitcast.9) | data formatting | bytes 81920
  36.7 0.6 %copy.9 = f32[128,128]{1,0:T(8,128)} copy(f32[128,128]{1,0:T(8,128)S(1)} %get-tuple-element.11) | data formatting | bytes 131072
Async XLA Ops:
  0.6 0.8 %copy-start = (f32[5,1,8,256]{3,2,1,0:T(8,128)S(1)}, f32[5,1,8,256]{3,2,1,0:T(8,128)}, u32[]{:S(2)}) copy-start(f32[5,1,8,256]{3,2,1,0:T(8,128)} %param.2) | copy-start | bytes 122884

commit v8 on v7

--- a/solution.py
+++ b/solution.py
@@ -200,7 +200,10 @@
         x = jnp.concatenate([modes[c, 0:keep, :], tail[c]], 0)
         return lax.dot_general(x, x, NT, preferred_element_type=jnp.float32)
 
+    early = comps // 2 + 1
     total = gram_part(0)
+    for c in range(1, early):
+        total = total + gram_part(c)
     pl.semaphore_wait(barrier, wide + narrow + 2)
 
     copies = halo_copies(0)
@@ -208,7 +211,7 @@
         copy.start()
     pending = list(copies)
 
-    for c in range(1, comps):
+    for c in range(early, comps):
         total = total + gram_part(c)
     gram[...] = total
     mine = pl.ds(pl.multiple_of(iw * piece_rows, piece_rows), piece_rows)

time: 37.5 us -> 37.5 us (level)
  no operation moved by 1% of the time
where the time goes in v8:
time: 37.5 us; the launch traced here: 37.3 us
  Pallas kernels  34.7 us (93%)
  local copies, waits for them, and re-layouts  2.02 us (5%)
  between operations  0.65 us (2%)
    pallas_call x1, Pallas kernels, local(): pl.pallas_call(functools.partial(kernel, wide, narrow), out_shape=(jax.Sh...  34.7 us
    unnamed x4, local copies, waits for them, and re-layouts  2.02 us

profile of v8, /device:TPU:0, one launch (start us, length us, event | category | flops | bytes accessed | tf_op | source)
XLA Modules:
  0.0 37.3 jit_solution(12141063252180539513)
XLA Ops:
  0.6 0.0 copy-start
  0.6 0.8 %copy-done = f32[5,1,8,256]{3,2,1,0:T(8,128)S(1)} copy-done((f32[5,1,8,256]{3,2,1,0:T(8,128)S(1)}, f32[5,1,8,256]{3,2,1,0:T(8,128)}, u32[]{:S(2)}) %copy-start) | copy-done | bytes 40984
  1.4 34.7 %shard_map.41 = (f32[5,8,256]{2,1,0:T(8,128)S(1)}, f32[128,128]{1,0:T(8,128)S(1)}) custom-call(f32[5,8,256]{2,1,0:T(8,128)S(1)} %bitcast.10, bf16[5,124,2048]{2,1,0:T(8,128)(2,1)} %bitcast.11), custom_call_target="tpu_custom_call" | custom-call | tf_op jit(solution)/shard_map/pallas_call | solution.py:470
  36.1 0.6 %copy.8 = f32[5,1,8,256]{3,2,1,0:T(8,128)} copy(f32[5,1,8,256]{3,2,1,0:T(8,128)S(1)} %bitcast.9) | data formatting | bytes 81920
  36.7 0.6 %copy.9 = f32[128,128]{1,0:T(8,128)} copy(f32[128,128]{1,0:T(8,128)S(1)} %get-tuple-element.11) | data formatting | bytes 131072
Async XLA Ops:
  0.6 0.8 %copy-start = (f32[5,1,8,256]{3,2,1,0:T(8,128)S(1)}, f32[5,1,8,256]{3,2,1,0:T(8,128)}, u32[]{:S(2)}) copy-start(f32[5,1,8,256]{3,2,1,0:T(8,128)} %param.2) | copy-start | bytes 122884
